TPU v7x, 128 devices: a whole 4x4x4 slice. The times are simulated.
128 devices in a mesh: depth: 4 (over z), row: 8 (over y, core), col: 4 (over x).
Axes of the slice: x: 4, y: 4, z: 4, core: 2. Of those that a mesh axis runs over, the one named last changes fastest.
Arguments:
- inputs: bfloat16 [1024, 12288], P(('depth', 'col'), 'row'), may hold values from -6 to 6
- w_in: bfloat16 [12288, 24576], P('row', ('depth', 'col')), may hold values from -0.0546875 to 0.0546875
- w_out: bfloat16 [24576, 12288], P(('depth', 'col'), 'row'), may hold values from -0.01953125 to 0.01953125
- out_grad: bfloat16 [1024, 12288], P(('depth', 'col'), 'row'), may hold values from -6 to 6
Outputs:
- outputs: bfloat16 [1024, 12288], P(('depth', 'col'), 'row')
- in_grad: bfloat16 [1024, 12288], P(('depth', 'col'), 'row')
All inputs are finite; a program needn't handle non-finite values.
Results may differ from a plain program's by a relative error of at most 0.009.
Values may be sent and summed in bfloat16 or wider, within the bound.
No kernel may reach another device: no remote copies, remote signals or barrier semaphores. Data moves between devices by JAX's collectives and lax.ppermute only.
A program may use at most 128 MiB of HBM per device.

v0:
```python
import jax
import jax.numpy as jnp
from jax import lax
from jax.sharding import PartitionSpec as P

curve = 0.7978845608028654
cubic = 0.044715


def gelu_value(value):
    tangent = jnp.tanh(curve * (value + cubic * value * value * value))
    return 0.5 * value * (1.0 + tangent)


def gelu_slope(value):
    tangent = jnp.tanh(curve * (value + cubic * value * value * value))
    return 0.5 * (1.0 + tangent) + 0.5 * value * (1.0 - tangent * tangent) * curve * (
        1.0 + 3.0 * cubic * value * value
    )


def transposed(left, right):
    return lax.dot_general(
        left, right, (((1,), (1,)), ((), ())), preferred_element_type=jnp.float32
    )


def shards(inputs, w_in, w_out, out_grad):
    pre_terms = jnp.dot(
        lax.all_gather(inputs, ("depth", "col"), axis=0, tiled=True),
        w_in,
        preferred_element_type=jnp.float32,
    )
    pre = lax.psum_scatter(pre_terms, "row", scatter_dimension=0, tiled=True)
    act = gelu_value(pre).astype(jnp.bfloat16)
    out_terms = jnp.dot(
        lax.all_gather(act, "row", axis=0, tiled=True), w_out, preferred_element_type=jnp.float32
    )
    outputs = lax.psum_scatter(out_terms, ("depth", "col"), scatter_dimension=0, tiled=True).astype(
        jnp.bfloat16
    )
    grad_terms = transposed(lax.all_gather(out_grad, ("depth", "col"), axis=0, tiled=True), w_out)
    grad_act = lax.psum_scatter(grad_terms, "row", scatter_dimension=0, tiled=True)
    grad_pre = (grad_act * gelu_slope(pre)).astype(jnp.bfloat16)
    input_terms = transposed(lax.all_gather(grad_pre, "row", axis=0, tiled=True), w_in)
    in_grad = lax.psum_scatter(
        input_terms, ("depth", "col"), scatter_dimension=0, tiled=True
    ).astype(jnp.bfloat16)
    return (outputs, in_grad)


def solution(mesh):
    in_specs = (
        P(("depth", "col"), "row"),
        P("row", ("depth", "col")),
        P(("depth", "col"), "row"),
        P(("depth", "col"), "row"),
    )
    out_specs = (P(("depth", "col"), "row"), P(("depth", "col"), "row"))
    return jax.shard_map(shards, mesh=mesh, in_specs=in_specs, out_specs=out_specs, check_vma=False)
```

profile of v0, /device:TPU:0, one launch (start us, length us, event | category | flops | bytes accessed | tf_op | source)
XLA Modules:
  0.0 435.5 jit_solution(6055639819352021573)
XLA Ops:
  7.2 0.7 all-gather.5.cloned.1.call-update
  7.9 0.7 all-gather.9.cloned.1.call-update
  8.6 0.0 reduce-scatter.5.cloned.1.call-start
  8.7 52.0 %all-gather.5.cloned.1.call-done = bf16[1024,1536]{1,0:T(8,128)(2,1)} async-done(((bf16[64,1536]{1,0:T(8,128)(2,1)}), bf16[1024,1536]{1,0:T(8,128)(2,1)}) %all-gather.5.cloned.1.call-update) | async-done | bytes 3145744 | tf_op jit(solution)/shard_map/all_gather | solution.py:30
  60.7 9.7 %fusion.7 = f32[1024,1536]{1,0:T(8,128)} fusion(bf16[1024,1536]{1,0:T(8,128)(2,1)} %all-gather.5.cloned.1.call-done, bf16[1536,1536]{1,0:T(8,128)(2,1)} %param.5), kind=kOutput, calls=%fused_computation.10 | convolution fusion | flops 4831838208 | bytes 14155776 | tf_op jit(solution)/shard_map/dot_general | solution.py:29
  70.4 0.0 reduce-scatter.9.cloned.1.call-start
  70.5 39.3 %all-gather.9.cloned.1.call-done = bf16[1024,1536]{1,0:T(8,128)(2,1)} async-done(((bf16[64,1536]{1,0:T(8,128)(2,1)}), bf16[1024,1536]{1,0:T(8,128)(2,1)}) %all-gather.9.cloned.1.call-update) | async-done | bytes 3145744 | tf_op jit(solution)/shard_map/all_gather | solution.py:42
  109.8 9.7 %fusion.9 = f32[1024,1536]{1,0:T(8,128)} fusion(bf16[1024,1536]{1,0:T(8,128)(2,1)} %all-gather.9.cloned.1.call-done, bf16[1536,1536]{1,0:T(8,128)(2,1)} %param.6), kind=kOutput, calls=%fused_computation.12 | convolution fusion | flops 4831838208 | bytes 14155776 | tf_op jit(solution)/shard_map/dot_general | solution.py:23
  119.5 0.0 all-gather.7.cloned.1.call-start
  119.6 33.9 %reduce-scatter.5.cloned.1.call-done = f32[128,1536]{1,0:T(8,128)} async-done(((f32[1024,1536]{1,0:T(8,128)}), f32[128,1536]{1,0:T(8,128)}) %reduce-scatter.5.cloned.1.call-update) | async-done | bytes 786448 | tf_op jit(solution)/shard_map/reduce_scatter | solution.py:34
  153.5 44.5 %reduce-scatter.9.cloned.1.call-done = f32[128,1536]{1,0:T(8,128)} async-done(((f32[1024,1536]{1,0:T(8,128)}), f32[128,1536]{1,0:T(8,128)}) %reduce-scatter.9.cloned.1.call-update) | async-done | bytes 786448 | tf_op jit(solution)/shard_map/reduce_scatter | solution.py:43
  198.0 2.8 fusion.6
  200.8 0.0 all-gather.11.cloned.1.call-start
  200.9 0.5 all-gather.11.cloned.1.call-update
  201.4 0.0 reduce-scatter.7.cloned.1.call-start
  201.5 27.0 %all-gather.7.cloned.1.call-done = bf16[1024,1536]{1,0:T(8,128)(2,1)} async-done(((bf16[128,1536]{1,0:T(8,128)(2,1)}), bf16[1024,1536]{1,0:T(8,128)(2,1)}) %all-gather.7.cloned.1.call-update) | async-done | bytes 3145744 | tf_op jit(solution)/shard_map/all_gather | solution.py:37
  228.5 9.7 %fusion.8 = f32[1024,1536]{1,0:T(8,128)} fusion(bf16[1024,1536]{1,0:T(8,128)(2,1)} %all-gather.7.cloned.1.call-done, bf16[1536,1536]{1,0:T(8,128)(2,1)} %param.6), kind=kOutput, calls=%fused_computation.11 | convolution fusion | flops 4831838208 | bytes 14155776 | tf_op jit(solution)/shard_map/dot_general | solution.py:36
  238.2 0.0 reduce-scatter.11.cloned.1.call-start
  238.2 19.6 %all-gather.11.cloned.1.call-done = bf16[1024,1536]{1,0:T(8,128)(2,1)} async-done(((bf16[128,1536]{1,0:T(8,128)(2,1)}), bf16[1024,1536]{1,0:T(8,128)(2,1)}) %all-gather.11.cloned.1.call-update) | async-done | bytes 3145744 | tf_op jit(solution)/shard_map/all_gather | solution.py:45
  257.8 9.7 %fusion.10 = f32[1024,1536]{1,0:T(8,128)} fusion(bf16[1024,1536]{1,0:T(8,128)(2,1)} %all-gather.11.cloned.1.call-done, bf16[1536,1536]{1,0:T(8,128)(2,1)} %param.5), kind=kOutput, calls=%fused_computation.13 | convolution fusion | flops 4831838208 | bytes 14155776 | tf_op jit(solution)/shard_map/dot_general | solution.py:23
  267.6 75.3 %reduce-scatter.7.cloned.1.call-done = f32[64,1536]{1,0:T(8,128)} async-done(((f32[1024,1536]{1,0:T(8,128)}), f32[64,1536]{1,0:T(8,128)}) %reduce-scatter.7.cloned.1.call-update) | async-done | bytes 393232 | tf_op jit(solution)/shard_map/reduce_scatter | solution.py:39
  342.9 1.7 convert_element_type.13
  344.5 82.4 %reduce-scatter.11.cloned.1.call-done = f32[64,1536]{1,0:T(8,128)} async-done(((f32[1024,1536]{1,0:T(8,128)}), f32[64,1536]{1,0:T(8,128)}) %reduce-scatter.11.cloned.1.call-update) | async-done | bytes 393232 | tf_op jit(solution)/shard_map/reduce_scatter | solution.py:46
  427.0 1.7 convert_element_type.15
  (7 shorter events, 0.2 us)
Async XLA Ops:
  7.2 53.5 %all-gather.5.cloned.1.call-start = ((), (), s32[]{:S(2)}) async-start(), calls=%async_computation.4 | async-start | bytes 3342336 | tf_op jit(solution)/shard_map/all_gather | solution.py:30
  7.9 101.9 %all-gather.9.cloned.1.call-start = ((), (), s32[]{:S(2)}) async-start(), calls=%async_computation.8 | async-start | bytes 3342336 | tf_op jit(solution)/shard_map/all_gather | solution.py:42
  8.6 144.9 %reduce-scatter.5.cloned.1.call-start = ((), (), s32[]{:S(2)}) async-start(), calls=%async_computation.5 | async-start | bytes 7077888 | tf_op jit(solution)/shard_map/reduce_scatter | solution.py:34
  70.4 127.6 %reduce-scatter.9.cloned.1.call-start = ((), (), s32[]{:S(2)}) async-start(), calls=%async_computation.9 | async-start | bytes 7077888 | tf_op jit(solution)/shard_map/reduce_scatter | solution.py:43
  119.5 108.9 %all-gather.7.cloned.1.call-start = ((), (), s32[]{:S(2)}) async-start(), calls=%async_computation.6 | async-start | bytes 3538944 | tf_op jit(solution)/shard_map/all_gather | solution.py:37
  200.8 57.0 %all-gather.11.cloned.1.call-start = ((), (), s32[]{:S(2)}) async-start(), calls=%async_computation.10 | async-start | bytes 3538944 | tf_op jit(solution)/shard_map/all_gather | solution.py:45
  201.4 141.4 %reduce-scatter.7.cloned.1.call-start = ((), (), s32[]{:S(2)}) async-start(), calls=%async_computation.7 | async-start | bytes 6684672 | tf_op jit(solution)/shard_map/reduce_scatter | solution.py:39
  238.2 188.8 %reduce-scatter.11.cloned.1.call-start = ((), (), s32[]{:S(2)}) async-start(), calls=%async_computation.11 | async-start | bytes 6684672 | tf_op jit(solution)/shard_map/reduce_scatter | solution.py:46
Sparse Core Ops, SparseCore 0:
  10.1 50.5 all-gather.4
  62.8 46.8 all-gather.8
  112.2 41.2 reduce-scatter.4
  155.8 42.1 reduce-scatter.8
  200.9 27.4 all-gather.6
  230.0 27.7 all-gather.10
  261.3 81.5 reduce-scatter.6
  346.3 80.6 reduce-scatter.10
where the time goes:
time: 436 us
  waiting for transfers between devices  376 us (86%)
  matrix products  38.9 us (9%)
  between operations  14.1 us (3%)
  other arithmetic  6.18 us (1%)
    reduce_scatter x1, waiting for transfers between devices, shards(): lax.psum_scatter(input_terms, ('depth', 'col'), scatter_dimension=0, tile...  82.4 us
    reduce_scatter x1, waiting for transfers between devices, shards(): lax.psum_scatter(out_terms, ('depth', 'col'), scatter_dimension=0, tiled=...  75.3 us
    all_gather x1, waiting for transfers between devices, shards(): lax.all_gather(inputs, ('depth', 'col'), axis=0, tiled=True)  52 us
    reduce_scatter x1, waiting for transfers between devices, shards(): lax.psum_scatter(grad_terms, 'row', scatter_dimension=0, tiled=True)  44.5 us
    all_gather x1, waiting for transfers between devices, shards(): lax.all_gather(out_grad, ('depth', 'col'), axis=0, tiled=True)  39.3 us
    reduce_scatter x1, waiting for transfers between devices, shards(): pre = lax.psum_scatter(pre_terms, 'row', scatter_dimension=0, tiled=True)  33.9 us
    all_gather x1, waiting for transfers between devices, shards(): lax.all_gather(act, 'row', axis=0, tiled=True)  27 us
    all_gather x1, waiting for transfers between devices, shards(): lax.all_gather(grad_pre, 'row', axis=0, tiled=True)  19.6 us
  transfers between devices with their start and end apart: 8, of which 8 were waited for; matrix products, arithmetic and copies ran while one was open for 9% of the time, Pallas kernels for 0%

commit v1 on v0

v1 whole, which is shorter than its diff:
```python
import functools

import jax
import jax.numpy as jnp
from jax import lax
from jax.experimental import pallas as pl
from jax.experimental.pallas import tpu as pltpu
from jax.sharding import PartitionSpec as P

curve = 0.7978845608028654
cubic = 0.044715
AXES = ("depth", "row", "col")
BLOCK = 64


def gelu_value(value):
    tangent = jnp.tanh(curve * (value + cubic * value * value * value))
    return 0.5 * value * (1.0 + tangent)


def gelu_slope(value):
    tangent = jnp.tanh(curve * (value + cubic * value * value * value))
    return 0.5 * (1.0 + tangent) + 0.5 * value * (1.0 - tangent * tangent) * curve * (
        1.0 + 3.0 * cubic * value * value
    )


def device_pairs(move):
    pairs = []
    for z in range(4):
        for r in range(8):
            for x in range(4):
                to_z, to_y, to_core, to_x = move(z, r // 2, r % 2, x)
                source = z * 32 + r * 4 + x
                target = (to_z % 4) * 32 + ((to_y % 4) * 2 + to_core) * 4 + to_x % 4
                pairs.append((source, target))
    return pairs


def send(value, move):
    return lax.ppermute(value, AXES, device_pairs(move))


def first_axis(k):
    return lambda z, y, core, x: (z + k * core, y, core, x + k * (1 - core))


def second_axis(k):
    return lambda z, y, core, x: (z + k * (1 - core), y, core, x + k * core)


def along_y(k):
    return lambda z, y, core, x: (z, y + k, core, x)


def other_core(z, y, core, x):
    return (z, y, 1 - core, x)


def matmul_kernel(place, transposed, counts, pieces, sizes, *refs):
    sources = refs[:pieces]
    weight = refs[pieces]
    outs = refs[pieces + 1 : -2]
    rows, arrived = refs[-2:]

    @pl.when(pl.program_id(0) == 0)
    def _():
        row = lax.axis_index("row")
        core, y = lax.rem(row, 2), lax.div(row, 2)
        copies = []
        for piece, source in enumerate(sources):
            for block in range(counts):
                at = pl.multiple_of(place(piece, block, core, y) * BLOCK, BLOCK)
                copies.append(
                    pltpu.make_async_copy(
                        source.at[pl.ds(block * BLOCK, BLOCK)],
                        rows.at[pl.ds(at, BLOCK)],
                        arrived.at[len(copies)],
                    )
                )
        for copy in copies:
            copy.start()
        for copy in copies:
            copy.wait()

    contract = 1 if transposed else 0
    product = lax.dot_general(
        rows[...],
        weight[...],
        (((1,), (contract,)), ((), ())),
        preferred_element_type=jnp.float32,
    ).astype(jnp.bfloat16)
    start = 0
    for out, size in zip(outs, sizes):
        out[...] = product[start : start + size]
        start += size


def matmul(sources, weight, transposed, place, sizes, tile=256):
    depth = weight.shape[1] if transposed else weight.shape[0]
    width = weight.shape[0] if transposed else weight.shape[1]
    total = sum(sizes)
    counts = sources[0].shape[0] // BLOCK
    if transposed:
        weight_spec = pl.BlockSpec((tile, depth), lambda j: (j, 0))
    else:
        weight_spec = pl.BlockSpec((depth, tile), lambda j: (0, j))
    return pl.pallas_call(
        functools.partial(matmul_kernel, place, transposed, counts, len(sources), sizes),
        grid=(width // tile,),
        out_shape=[jax.ShapeDtypeStruct((size, width), jnp.bfloat16) for size in sizes],
        in_specs=[pl.BlockSpec(memory_space=pl.ANY)] * len(sources) + [weight_spec],
        out_specs=[pl.BlockSpec((size, tile), lambda j: (0, j)) for size in sizes],
        scratch_shapes=[
            pltpu.VMEM((total, depth), jnp.bfloat16),
            pltpu.SemaphoreType.DMA((total // BLOCK,)),
        ],
        compiler_params=pltpu.CompilerParams(vmem_limit_bytes=24 * 2**20),
        cost_estimate=pl.CostEstimate(
            flops=2 * total * depth * width,
            bytes_accessed=2 * (total * depth + depth * width + total * width),
            transcendentals=0,
        ),
    )(*sources, weight)


def place_terms(piece, block, core, y):
    dz = jnp.where(core == 0, piece, block)
    dx = jnp.where(core == 0, block, piece)
    half, step = lax.div(dz, 2), lax.rem(dz, 2)
    kept = jnp.where(half == core, 1, 0)
    return kept * 8 + lax.rem(dx - y + 4, 4) * 2 + step


def place_sums(piece, block, core, y):
    half = core if piece < 4 else 1 - core
    dz = 2 * half + block
    dx = lax.rem(y + piece % 4, 4)
    return jnp.where(core == 0, dz * 4 + dx, dx * 4 + dz)


def gather_tokens(own):
    near = [own] + [send(own, first_axis(-k)) for k in (1, 2, 3)]
    line = jnp.concatenate(near)
    return [line] + [send(line, second_axis(-k)) for k in (1, 2, 3)]


def sum_parts(parts):
    total = parts[0].astype(jnp.float32)
    for part in parts[1:]:
        total = total + part.astype(jnp.float32)
    return total


def reduce_rows(passed, kept):
    both = sum_parts([kept, send(passed, other_core)]).astype(jnp.bfloat16)
    quarters = [both[k * 128 : (k + 1) * 128] for k in range(4)]
    return sum_parts([quarters[0]] + [send(quarters[k], along_y(k)) for k in (1, 2, 3)])


def gather_rows(own):
    mine = [own] + [send(own, along_y(-k)) for k in (1, 2, 3)]
    return mine + [send(part, other_core) for part in mine]


def reduce_tokens(groups):
    line = sum_parts([groups[0]] + [send(groups[k], second_axis(k)) for k in (1, 2, 3)])
    line = line.astype(jnp.bfloat16)
    blocks = [line[k * BLOCK : (k + 1) * BLOCK] for k in range(4)]
    total = sum_parts([blocks[0]] + [send(blocks[k], first_axis(k)) for k in (1, 2, 3)])
    return total.astype(jnp.bfloat16)


def shards(inputs, w_in, w_out, out_grad):
    pre = reduce_rows(*matmul(gather_tokens(inputs), w_in, False, place_terms, [512, 512]))
    grad_act = reduce_rows(*matmul(gather_tokens(out_grad), w_out, True, place_terms, [512, 512]))
    act = gelu_value(pre).astype(jnp.bfloat16)
    grad_pre = (grad_act * gelu_slope(pre)).astype(jnp.bfloat16)
    outputs = reduce_tokens(matmul(gather_rows(act), w_out, False, place_sums, [256] * 4))
    in_grad = reduce_tokens(matmul(gather_rows(grad_pre), w_in, True, place_sums, [256] * 4))
    return (outputs, in_grad)


def solution(mesh):
    in_specs = (
        P(("depth", "col"), "row"),
        P("row", ("depth", "col")),
        P(("depth", "col"), "row"),
        P(("depth", "col"), "row"),
    )
    out_specs = (P(("depth", "col"), "row"), P(("depth", "col"), "row"))
    return jax.shard_map(shards, mesh=mesh, in_specs=in_specs, out_specs=out_specs, check_vma=False)
```

time: 436 us -> 222 us (0.51)
  waiting for transfers between devices: 376 us -> 92.6 us
  starting transfers between devices: 0.32 us -> 74.9 us
  Pallas kernels: 0 us -> 45.3 us
  matrix products: 38.9 us -> 0 us
  between operations: 14.1 us -> 0.91 us
    reduce_scatter x4 -> x0, waiting for transfers between devices: 236 us -> none  [the longest x1 82.4 us: shards(): lax.psum_scatter(input_terms, ('depth', 'col'), scatter_dimension=0, tile...]
    all_gather x4 -> x0, waiting for transfers between devices: 138 us -> none  [the longest x1 52 us: shards(): lax.all_gather(inputs, ('depth', 'col'), axis=0, tiled=True)]
    ppermute x0 -> x46, waiting for transfers between devices: none -> 92.6 us  [send(): return lax.ppermute(value, AXES, device_pairs(move))]
    ppermute x0 -> x46, starting transfers between devices: none -> 74.9 us  [send(): return lax.ppermute(value, AXES, device_pairs(move))]
    pallas_call x0 -> x4, Pallas kernels: none -> 45.3 us  [matmul(): pl.pallas_call(functools.partial(matmul_kernel, place, transposed, counts...]
    dot_general x4 -> x0, matrix products: 38.9 us -> none  [the longest x2 19.5 us: transposed(): lax.dot_general(left, right, (((1,), (1,)), ((), ())), preferred_element_...]
  transfers between devices with their start and end apart: 8 -> 46, of which waited for: 8 -> 17; matrix products, arithmetic and copies ran while one was open for 9% -> 2% of each run, Pallas kernels for 0% -> 20%
where the time goes in v1:
time: 222 us; the launch traced here: 221 us
  waiting for transfers between devices  92.6 us (42%)
  starting transfers between devices  74.9 us (34%)
  Pallas kernels  45.3 us (20%)
  other arithmetic  4.01 us (2%)
  local copies, waits for them, and re-layouts  3.66 us (2%)
    ppermute x46, waiting for transfers between devices, send(): return lax.ppermute(value, AXES, device_pairs(move))  92.6 us
    ppermute x46, starting transfers between devices, send(): return lax.ppermute(value, AXES, device_pairs(move))  74.9 us
    pallas_call x4, Pallas kernels, matmul(): pl.pallas_call(functools.partial(matmul_kernel, place, transposed, counts...  45.3 us
  transfers between devices with their start and end apart: 46, of which 17 were waited for; matrix products, arithmetic and copies ran while one was open for 2% of the time, Pallas kernels for 20%

profile of v1, /device:TPU:0, one launch (start us, length us, event | category | flops | bytes accessed | tf_op | source)
XLA Modules:
  0.0 221.4 jit_solution(17067003923976936186)
XLA Ops:
  0.6 2.9 %collective-permute-start = (bf16[64,1536]{1,0:T(8,128)(2,1)}, bf16[64,1536]{1,0:T(8,128)(2,1)S(1)}, u32[]{:S(2)}, u32[]{:S(2)}) collective-permute-start(bf16[64,1536]{1,0:T(8,128)(2,1)} %param.4), channel_id=1, source_target_pairs={{0,3},{1,0},{2,1},{3,2},{4,100},{5,101},{6,102},{7,103},{8,11},{9,... | collective-permute-start | bytes 589832 | tf_op jit(solution)/shard_map/ppermute | solution.py:41
  13.1 4.1 %collective-permute-start.3 = (bf16[256,1536]{1,0:T(8,128)(2,1)S(1)}, bf16[256,1536]{1,0:T(8,128)(2,1)S(1)}, u32[]{:S(2)}, u32[]{:S(2)}) collective-permute-start(bf16[256,1536]{1,0:T(8,128)(2,1)S(1)} %constant_dynamic-update-slice_fusion.refs_0_), channel_id=1, source_target_pairs={{0,96},{1,97},{2,98},{3,99},{4,7},{5,4},{6,5},{7,6},{8,104},{9,105... | collective-permute-start | bytes 2359304 | tf_op jit(solution)/shard_map/ppermute | solution.py:41
  18.6 14.1 %collective-permute-done.25 = bf16[64,1536]{1,0:T(8,128)(2,1)S(1)} collective-permute-done((bf16[64,1536]{1,0:T(8,128)(2,1)S(1)}, bf16[64,1536]{1,0:T(8,128)(2,1)S(1)}, u32[]{:S(2)}, u32[]{:S(2)}) %collective-permute-start.25) | collective-permute-done | bytes 196640 | tf_op jit(solution)/shard_map/ppermute | solution.py:41
  35.1 4.0 %collective-permute-done.5.refs_3_ = bf16[256,1536]{1,0:T(8,128)(2,1)S(1)} collective-permute-done((bf16[256,1536]{1,0:T(8,128)(2,1)S(1)}, bf16[256,1536]{1,0:T(8,128)(2,1)S(1)}, u32[]{:S(2)}, u32[]{:S(2)}) %collective-permute-start.5) | collective-permute-done | bytes 786464 | tf_op jit(solution)/shard_map/ppermute | solution.py:41
  41.5 11.4 %shard_map.59 = (bf16[512,1536]{1,0:T(8,128)(2,1)S(1)}, bf16[512,1536]{1,0:T(8,128)(2,1)S(1)}) custom-call(bf16[256,1536]{1,0:T(8,128)(2,1)S(1)} %constant_dynamic-update-slice_fusion.refs_0_, bf16[256,1536]{1,0:T(8,128)(2,1)S(1)} %collective-permute-done.3.refs_1_, bf16[256,1536]{1,0:T(8,128)(2,1)S(1)} %collective-permute-done.4.refs_2_, ...), custom_call_target="tpu_custom_call" | custom-call | flops 4831838208 | bytes 11010048 | tf_op jit(solution)/shard_map/pallas_call | solution.py:108
  53.0 2.9 %collective-permute-done.28.refs_3_ = bf16[256,1536]{1,0:T(8,128)(2,1)S(1)} collective-permute-done((bf16[256,1536]{1,0:T(8,128)(2,1)S(1)}, bf16[256,1536]{1,0:T(8,128)(2,1)S(1)}, u32[]{:S(2)}, u32[]{:S(2)}) %collective-permute-start.28) | collective-permute-done | bytes 786464 | tf_op jit(solution)/shard_map/ppermute | solution.py:41
  56.0 11.2 %shard_map.61 = (bf16[512,1536]{1,0:T(8,128)(2,1)S(1)}, bf16[512,1536]{1,0:T(8,128)(2,1)S(1)}) custom-call(bf16[256,1536]{1,0:T(8,128)(2,1)S(1)} %constant_dynamic-update-slice_fusion.4.refs_0_, bf16[256,1536]{1,0:T(8,128)(2,1)S(1)} %collective-permute-done.26.refs_1_, bf16[256,1536]{1,0:T(8,128)(2,1)S(1)} %collective-permute-done.27.refs_2_, ...), custom_call_target="tpu_custom_call" | custom-call | flops 4831838208 | bytes 11010048 | tf_op jit(solution)/shard_map/pallas_call | solution.py:108
  69.5 2.9 %collective-permute-start.8 = (bf16[128,1536]{1,0:T(8,128)(2,1)S(1)}, bf16[128,1536]{1,0:T(8,128)(2,1)S(1)}, u32[]{:S(2)}, u32[]{:S(2)}) collective-permute-start(bf16[128,1536]{1,0:T(8,128)(2,1)S(1)} %get-tuple-element.33), channel_id=1, source_target_pairs={{0,16},{1,17},{2,18},{3,19},{4,20},{5,21},{6,22},{7,23},{8,24},{9,... | collective-permute-start | bytes 1179656 | tf_op jit(solution)/shard_map/ppermute | solution.py:41
  75.8 5.2 %collective-permute-done.7 = bf16[128,1536]{1,0:T(8,128)(2,1)S(1)} collective-permute-done((bf16[128,1536]{1,0:T(8,128)(2,1)S(1)}, bf16[128,1536]{1,0:T(8,128)(2,1)S(1)}, u32[]{:S(2)}, u32[]{:S(2)}) %collective-permute-start.7) | collective-permute-done | bytes 393248 | tf_op jit(solution)/shard_map/ppermute | solution.py:41
  82.9 7.9 %collective-permute-done.8 = bf16[128,1536]{1,0:T(8,128)(2,1)S(1)} collective-permute-done((bf16[128,1536]{1,0:T(8,128)(2,1)S(1)}, bf16[128,1536]{1,0:T(8,128)(2,1)S(1)}, u32[]{:S(2)}, u32[]{:S(2)}) %collective-permute-start.8) | collective-permute-done | bytes 393248 | tf_op jit(solution)/shard_map/ppermute | solution.py:41
  90.8 6.7 %collective-permute-done.30 = bf16[128,1536]{1,0:T(8,128)(2,1)S(1)} collective-permute-done((bf16[128,1536]{1,0:T(8,128)(2,1)S(1)}, bf16[128,1536]{1,0:T(8,128)(2,1)S(1)}, u32[]{:S(2)}, u32[]{:S(2)}) %collective-permute-start.30) | collective-permute-done | bytes 393248 | tf_op jit(solution)/shard_map/ppermute | solution.py:41
  97.5 9.6 %collective-permute-done.31 = bf16[128,1536]{1,0:T(8,128)(2,1)S(1)} collective-permute-done((bf16[128,1536]{1,0:T(8,128)(2,1)S(1)}, bf16[128,1536]{1,0:T(8,128)(2,1)S(1)}, u32[]{:S(2)}, u32[]{:S(2)}) %collective-permute-start.31) | collective-permute-done | bytes 393248 | tf_op jit(solution)/shard_map/ppermute | solution.py:41
  112.1 2.5 %collective-permute-start.10 = (bf16[128,1536]{1,0:T(8,128)(2,1)S(1)}, bf16[128,1536]{1,0:T(8,128)(2,1)S(1)}, u32[]{:S(2)}, u32[]{:S(2)}) collective-permute-start(bf16[128,1536]{1,0:T(8,128)(2,1)S(1)} %get-tuple-element.27.refs_0_), channel_id=1, source_target_pairs={{0,24},{1,25},{2,26},{3,27},{4,28},{5,29},{6,30},{7,31},{8,0},{9,1... | collective-permute-start | bytes 1179656 | tf_op jit(solution)/shard_map/ppermute | solution.py:41
  114.6 13.4 %collective-permute-done.33.refs_1_ = bf16[128,1536]{1,0:T(8,128)(2,1)S(1)} collective-permute-done((bf16[128,1536]{1,0:T(8,128)(2,1)S(1)}, bf16[128,1536]{1,0:T(8,128)(2,1)S(1)}, u32[]{:S(2)}, u32[]{:S(2)}) %collective-permute-start.33) | collective-permute-done | bytes 393248 | tf_op jit(solution)/shard_map/ppermute | solution.py:41
  128.0 4.7 %collective-permute-start.12 = (bf16[128,1536]{1,0:T(8,128)(2,1)S(1)}, bf16[128,1536]{1,0:T(8,128)(2,1)S(1)}, u32[]{:S(2)}, u32[]{:S(2)}) collective-permute-start(bf16[128,1536]{1,0:T(8,128)(2,1)S(1)} %get-tuple-element.27.refs_0_), channel_id=1, source_target_pairs={{0,8},{1,9},{2,10},{3,11},{4,12},{5,13},{6,14},{7,15},{8,16},{9,17... | collective-permute-start | bytes 1179656 | tf_op jit(solution)/shard_map/ppermute | solution.py:41
  133.2 10.9 %collective-permute-done.10.refs_1_ = bf16[128,1536]{1,0:T(8,128)(2,1)S(1)} collective-permute-done((bf16[128,1536]{1,0:T(8,128)(2,1)S(1)}, bf16[128,1536]{1,0:T(8,128)(2,1)S(1)}, u32[]{:S(2)}, u32[]{:S(2)}) %collective-permute-start.10) | collective-permute-done | bytes 393248 | tf_op jit(solution)/shard_map/ppermute | solution.py:41
  144.6 3.0 %collective-permute-done.12.refs_3_ = bf16[128,1536]{1,0:T(8,128)(2,1)S(1)} collective-permute-done((bf16[128,1536]{1,0:T(8,128)(2,1)S(1)}, bf16[128,1536]{1,0:T(8,128)(2,1)S(1)}, u32[]{:S(2)}, u32[]{:S(2)}) %collective-permute-start.12) | collective-permute-done | bytes 393248 | tf_op jit(solution)/shard_map/ppermute | solution.py:41
  148.2 11.3 %shard_map.62 = (bf16[256,1536]{1,0:T(8,128)(2,1)S(1)}, bf16[256,1536]{1,0:T(8,128)(2,1)S(1)}, bf16[256,1536]{1,0:T(8,128)(2,1)S(1)}, bf16[256,1536]{1,0:T(8,128)(2,1)S(1)}) custom-call(bf16[128,1536]{1,0:T(8,128)(2,1)S(1)} %get-tuple-element.26.refs_0_, bf16[128,1536]{1,0:T(8,128)(2,1)S(1)} %collective-permute-done.33.refs_1_, ...), custom_call_target="tpu_custom_call" | custom-call | flops 4831838208 | bytes 11010048 | tf_op jit(solution)/shard_map/pallas_call | solution.py:108
  162.9 11.4 %shard_map.60 = (bf16[256,1536]{1,0:T(8,128)(2,1)S(1)}, bf16[256,1536]{1,0:T(8,128)(2,1)S(1)}, bf16[256,1536]{1,0:T(8,128)(2,1)S(1)}, bf16[256,1536]{1,0:T(8,128)(2,1)S(1)}) custom-call(bf16[128,1536]{1,0:T(8,128)(2,1)S(1)} %get-tuple-element.27.refs_0_, bf16[128,1536]{1,0:T(8,128)(2,1)S(1)} %collective-permute-done.10.refs_1_, ...), custom_call_target="tpu_custom_call" | custom-call | flops 4831838208 | bytes 11010048 | tf_op jit(solution)/shard_map/pallas_call | solution.py:108
  177.3 3.9 %collective-permute-done.40 = bf16[256,1536]{1,0:T(8,128)(2,1)S(1)} collective-permute-done((bf16[256,1536]{1,0:T(8,128)(2,1)S(1)}, bf16[256,1536]{1,0:T(8,128)(2,1)S(1)}, u32[]{:S(2)}, u32[]{:S(2)}) %collective-permute-start.40) | collective-permute-done | bytes 786464 | tf_op jit(solution)/shard_map/ppermute | solution.py:41
  183.7 8.3 %collective-permute-start.44 = (bf16[64,1536]{1,0:T(8,128)(2,1)S(1)}, bf16[64,1536]{1,0:T(8,128)(2,1)S(1)}, u32[]{:S(2)}, u32[]{:S(2)}) collective-permute-start(bf16[64,1536]{1,0:T(8,128)(2,1)S(1)} %get-tuple-element.36), channel_id=1, source_target_pairs={{0,2},{1,3},{2,0},{3,1},{4,68},{5,69},{6,70},{7,71},{8,10},{9,11},... | collective-permute-start | bytes 589832 | tf_op jit(solution)/shard_map/ppermute | solution.py:41
  192.0 18.2 %collective-permute-start.45 = (bf16[64,1536]{1,0:T(8,128)(2,1)S(1)}, bf16[64,1536]{1,0:T(8,128)(2,1)S(1)}, u32[]{:S(2)}, u32[]{:S(2)}) collective-permute-start(bf16[64,1536]{1,0:T(8,128)(2,1)S(1)} %get-tuple-element.35), channel_id=1, source_target_pairs={{0,3},{1,0},{2,1},{3,2},{4,100},{5,101},{6,102},{7,103},{8,11},{9,... | collective-permute-start | bytes 589832 | tf_op jit(solution)/shard_map/ppermute | solution.py:41
  210.7 2.4 %collective-permute-start.21 = (bf16[64,1536]{1,0:T(8,128)(2,1)S(1)}, bf16[64,1536]{1,0:T(8,128)(2,1)S(1)}, u32[]{:S(2)}, u32[]{:S(2)}) collective-permute-start(bf16[64,1536]{1,0:T(8,128)(2,1)S(1)} %get-tuple-element.39), channel_id=1, source_target_pairs={{0,2},{1,3},{2,0},{3,1},{4,68},{5,69},{6,70},{7,71},{8,10},{9,11},... | collective-permute-start | bytes 589832 | tf_op jit(solution)/shard_map/ppermute | solution.py:41
  214.8 5.0 %collective-permute-done.20 = bf16[64,1536]{1,0:T(8,128)(2,1)S(1)} collective-permute-done((bf16[64,1536]{1,0:T(8,128)(2,1)S(1)}, bf16[64,1536]{1,0:T(8,128)(2,1)S(1)}, u32[]{:S(2)}, u32[]{:S(2)}) %collective-permute-start.20) | collective-permute-done | bytes 196640 | tf_op jit(solution)/shard_map/ppermute | solution.py:41
  (102 shorter events, 42.6 us)
Async XLA Ops:
  13.1 22.0 %collective-permute-start.3 = (bf16[256,1536]{1,0:T(8,128)(2,1)S(1)}, bf16[256,1536]{1,0:T(8,128)(2,1)S(1)}, u32[]{:S(2)}, u32[]{:S(2)}) collective-permute-start(bf16[256,1536]{1,0:T(8,128)(2,1)S(1)} %constant_dynamic-update-slice_fusion.refs_0_), channel_id=1, source_target_pairs={{0,96},{1,97},{2,98},{3,99},{4,7},{5,4},{6,5},{7,6},{8,104},{9,105... | collective-permute-start | bytes 2359304 | tf_op jit(solution)/shard_map/ppermute | solution.py:41
  17.2 17.9 %collective-permute-start.4 = (bf16[256,1536]{1,0:T(8,128)(2,1)S(1)}, bf16[256,1536]{1,0:T(8,128)(2,1)S(1)}, u32[]{:S(2)}, u32[]{:S(2)}) collective-permute-start(bf16[256,1536]{1,0:T(8,128)(2,1)S(1)} %constant_dynamic-update-slice_fusion.refs_0_), channel_id=1, source_target_pairs={{0,64},{1,65},{2,66},{3,67},{4,6},{5,7},{6,4},{7,5},{8,72},{9,73},... | collective-permute-start | bytes 2359304 | tf_op jit(solution)/shard_map/ppermute | solution.py:41
  17.2 22.0 %collective-permute-start.5 = (bf16[256,1536]{1,0:T(8,128)(2,1)S(1)}, bf16[256,1536]{1,0:T(8,128)(2,1)S(1)}, u32[]{:S(2)}, u32[]{:S(2)}) collective-permute-start(bf16[256,1536]{1,0:T(8,128)(2,1)S(1)} %constant_dynamic-update-slice_fusion.refs_0_), channel_id=1, source_target_pairs={{0,32},{1,33},{2,34},{3,35},{4,5},{5,6},{6,7},{7,4},{8,40},{9,41},... | collective-permute-start | bytes 2359304 | tf_op jit(solution)/shard_map/ppermute | solution.py:41
  32.7 20.3 %collective-permute-start.26 = (bf16[256,1536]{1,0:T(8,128)(2,1)S(1)}, bf16[256,1536]{1,0:T(8,128)(2,1)S(1)}, u32[]{:S(2)}, u32[]{:S(2)}) collective-permute-start(bf16[256,1536]{1,0:T(8,128)(2,1)S(1)} %constant_dynamic-update-slice_fusion.4.refs_0_), channel_id=1, source_target_pairs={{0,96},{1,97},{2,98},{3,99},{4,7},{5,4},{6,5},{7,6},{8,104},{9,105... | collective-permute-start | bytes 2359304 | tf_op jit(solution)/shard_map/ppermute | solution.py:41
  33.6 19.4 %collective-permute-start.27 = (bf16[256,1536]{1,0:T(8,128)(2,1)S(1)}, bf16[256,1536]{1,0:T(8,128)(2,1)S(1)}, u32[]{:S(2)}, u32[]{:S(2)}) collective-permute-start(bf16[256,1536]{1,0:T(8,128)(2,1)S(1)} %constant_dynamic-update-slice_fusion.4.refs_0_), channel_id=1, source_target_pairs={{0,64},{1,65},{2,66},{3,67},{4,6},{5,7},{6,4},{7,5},{8,72},{9,73},... | collective-permute-start | bytes 2359304 | tf_op jit(solution)/shard_map/ppermute | solution.py:41
  35.1 20.9 %collective-permute-start.28 = (bf16[256,1536]{1,0:T(8,128)(2,1)S(1)}, bf16[256,1536]{1,0:T(8,128)(2,1)S(1)}, u32[]{:S(2)}, u32[]{:S(2)}) collective-permute-start(bf16[256,1536]{1,0:T(8,128)(2,1)S(1)} %constant_dynamic-update-slice_fusion.4.refs_0_), channel_id=1, source_target_pairs={{0,32},{1,33},{2,34},{3,35},{4,5},{5,6},{6,7},{7,4},{8,40},{9,41},... | collective-permute-start | bytes 2359304 | tf_op jit(solution)/shard_map/ppermute | solution.py:41
  69.5 21.3 %collective-permute-start.8 = (bf16[128,1536]{1,0:T(8,128)(2,1)S(1)}, bf16[128,1536]{1,0:T(8,128)(2,1)S(1)}, u32[]{:S(2)}, u32[]{:S(2)}) collective-permute-start(bf16[128,1536]{1,0:T(8,128)(2,1)S(1)} %get-tuple-element.33), channel_id=1, source_target_pairs={{0,16},{1,17},{2,18},{3,19},{4,20},{5,21},{6,22},{7,23},{8,24},{9,... | collective-permute-start | bytes 1179656 | tf_op jit(solution)/shard_map/ppermute | solution.py:41
  72.4 18.4 %collective-permute-start.9 = (bf16[128,1536]{1,0:T(8,128)(2,1)S(1)}, bf16[128,1536]{1,0:T(8,128)(2,1)S(1)}, u32[]{:S(2)}, u32[]{:S(2)}) collective-permute-start(bf16[128,1536]{1,0:T(8,128)(2,1)S(1)} %get-tuple-element.32), channel_id=1, source_target_pairs={{0,24},{1,25},{2,26},{3,27},{4,28},{5,29},{6,30},{7,31},{8,0},{9,1... | collective-permute-start | bytes 1179656 | tf_op jit(solution)/shard_map/ppermute | solution.py:41
  74.3 23.2 %collective-permute-start.30 = (bf16[128,1536]{1,0:T(8,128)(2,1)S(1)}, bf16[128,1536]{1,0:T(8,128)(2,1)S(1)}, u32[]{:S(2)}, u32[]{:S(2)}) collective-permute-start(bf16[128,1536]{1,0:T(8,128)(2,1)S(1)} %get-tuple-element.28), channel_id=1, source_target_pairs={{0,8},{1,9},{2,10},{3,11},{4,12},{5,13},{6,14},{7,15},{8,16},{9,17... | collective-permute-start | bytes 1179656 | tf_op jit(solution)/shard_map/ppermute | solution.py:41
  75.0 32.1 %collective-permute-start.31 = (bf16[128,1536]{1,0:T(8,128)(2,1)S(1)}, bf16[128,1536]{1,0:T(8,128)(2,1)S(1)}, u32[]{:S(2)}, u32[]{:S(2)}) collective-permute-start(bf16[128,1536]{1,0:T(8,128)(2,1)S(1)} %get-tuple-element.30), channel_id=1, source_target_pairs={{0,16},{1,17},{2,18},{3,19},{4,20},{5,21},{6,22},{7,23},{8,24},{9,... | collective-permute-start | bytes 1179656 | tf_op jit(solution)/shard_map/ppermute | solution.py:41
  81.0 26.1 %collective-permute-start.32 = (bf16[128,1536]{1,0:T(8,128)(2,1)S(1)}, bf16[128,1536]{1,0:T(8,128)(2,1)S(1)}, u32[]{:S(2)}, u32[]{:S(2)}) collective-permute-start(bf16[128,1536]{1,0:T(8,128)(2,1)S(1)} %get-tuple-element.29), channel_id=1, source_target_pairs={{0,24},{1,25},{2,26},{3,27},{4,28},{5,29},{6,30},{7,31},{8,0},{9,1... | collective-permute-start | bytes 1179656 | tf_op jit(solution)/shard_map/ppermute | solution.py:41
  108.0 20.0 %collective-permute-start.33 = (bf16[128,1536]{1,0:T(8,128)(2,1)S(1)}, bf16[128,1536]{1,0:T(8,128)(2,1)S(1)}, u32[]{:S(2)}, u32[]{:S(2)}) collective-permute-start(bf16[128,1536]{1,0:T(8,128)(2,1)S(1)} %get-tuple-element.26.refs_0_), channel_id=1, source_target_pairs={{0,24},{1,25},{2,26},{3,27},{4,28},{5,29},{6,30},{7,31},{8,0},{9,1... | collective-permute-start | bytes 1179656 | tf_op jit(solution)/shard_map/ppermute | solution.py:41
  111.3 21.3 %collective-permute-start.35 = (bf16[128,1536]{1,0:T(8,128)(2,1)S(1)}, bf16[128,1536]{1,0:T(8,128)(2,1)S(1)}, u32[]{:S(2)}, u32[]{:S(2)}) collective-permute-start(bf16[128,1536]{1,0:T(8,128)(2,1)S(1)} %get-tuple-element.26.refs_0_), channel_id=1, source_target_pairs={{0,8},{1,9},{2,10},{3,11},{4,12},{5,13},{6,14},{7,15},{8,16},{9,17... | collective-permute-start | bytes 1179656 | tf_op jit(solution)/shard_map/ppermute | solution.py:41
  112.1 20.6 %collective-permute-start.36 = (bf16[128,1536]{1,0:T(8,128)(2,1)S(1)}, bf16[128,1536]{1,0:T(8,128)(2,1)S(1)}, u32[]{:S(2)}, u32[]{:S(2)}) collective-permute-start(bf16[128,1536]{1,0:T(8,128)(2,1)S(1)} %get-tuple-element.26.refs_0_), channel_id=1, source_target_pairs={{0,4},{1,5},{2,6},{3,7},{4,0},{5,1},{6,2},{7,3},{8,12},{9,13},{10,... | collective-permute-start | bytes 1179656 | tf_op jit(solution)/shard_map/ppermute | solution.py:41
  112.1 32.0 %collective-permute-start.10 = (bf16[128,1536]{1,0:T(8,128)(2,1)S(1)}, bf16[128,1536]{1,0:T(8,128)(2,1)S(1)}, u32[]{:S(2)}, u32[]{:S(2)}) collective-permute-start(bf16[128,1536]{1,0:T(8,128)(2,1)S(1)} %get-tuple-element.27.refs_0_), channel_id=1, source_target_pairs={{0,24},{1,25},{2,26},{3,27},{4,28},{5,29},{6,30},{7,31},{8,0},{9,1... | collective-permute-start | bytes 1179656 | tf_op jit(solution)/shard_map/ppermute | solution.py:41
  128.0 19.6 %collective-permute-start.12 = (bf16[128,1536]{1,0:T(8,128)(2,1)S(1)}, bf16[128,1536]{1,0:T(8,128)(2,1)S(1)}, u32[]{:S(2)}, u32[]{:S(2)}) collective-permute-start(bf16[128,1536]{1,0:T(8,128)(2,1)S(1)} %get-tuple-element.27.refs_0_), channel_id=1, source_target_pairs={{0,8},{1,9},{2,10},{3,11},{4,12},{5,13},{6,14},{7,15},{8,16},{9,17... | collective-permute-start | bytes 1179656 | tf_op jit(solution)/shard_map/ppermute | solution.py:41
  159.5 21.7 %collective-permute-start.40 = (bf16[256,1536]{1,0:T(8,128)(2,1)S(1)}, bf16[256,1536]{1,0:T(8,128)(2,1)S(1)}, u32[]{:S(2)}, u32[]{:S(2)}) collective-permute-start(bf16[256,1536]{1,0:T(8,128)(2,1)S(1)} %get-tuple-element.23), channel_id=1, source_target_pairs={{0,32},{1,33},{2,34},{3,35},{4,5},{5,6},{6,7},{7,4},{8,40},{9,41},... | collective-permute-start | bytes 2359304 | tf_op jit(solution)/shard_map/ppermute | solution.py:41
  159.6 21.6 %collective-permute-start.41 = (bf16[256,1536]{1,0:T(8,128)(2,1)S(1)}, bf16[256,1536]{1,0:T(8,128)(2,1)S(1)}, u32[]{:S(2)}, u32[]{:S(2)}) collective-permute-start(bf16[256,1536]{1,0:T(8,128)(2,1)S(1)} %get-tuple-element.24), channel_id=1, source_target_pairs={{0,64},{1,65},{2,66},{3,67},{4,6},{5,7},{6,4},{7,5},{8,72},{9,73},... | collective-permute-start | bytes 2359304 | tf_op jit(solution)/shard_map/ppermute | solution.py:41
  161.7 20.4 %collective-permute-start.42 = (bf16[256,1536]{1,0:T(8,128)(2,1)S(1)}, bf16[256,1536]{1,0:T(8,128)(2,1)S(1)}, u32[]{:S(2)}, u32[]{:S(2)}) collective-permute-start(bf16[256,1536]{1,0:T(8,128)(2,1)S(1)} %get-tuple-element.25), channel_id=1, source_target_pairs={{0,96},{1,97},{2,98},{3,99},{4,7},{5,4},{6,5},{7,6},{8,104},{9,105... | collective-permute-start | bytes 2359304 | tf_op jit(solution)/shard_map/ppermute | solution.py:41
  175.2 35.0 %collective-permute-start.18 = (bf16[256,1536]{1,0:T(8,128)(2,1)S(1)}, bf16[256,1536]{1,0:T(8,128)(2,1)S(1)}, u32[]{:S(2)}, u32[]{:S(2)}) collective-permute-start(bf16[256,1536]{1,0:T(8,128)(2,1)S(1)} %get-tuple-element.18), channel_id=1, source_target_pairs={{0,64},{1,65},{2,66},{3,67},{4,6},{5,7},{6,4},{7,5},{8,72},{9,73},... | collective-permute-start | bytes 2359304 | tf_op jit(solution)/shard_map/ppermute | solution.py:41
  181.2 29.0 %collective-permute-start.19 = (bf16[256,1536]{1,0:T(8,128)(2,1)S(1)}, bf16[256,1536]{1,0:T(8,128)(2,1)S(1)}, u32[]{:S(2)}, u32[]{:S(2)}) collective-permute-start(bf16[256,1536]{1,0:T(8,128)(2,1)S(1)} %get-tuple-element.19), channel_id=1, source_target_pairs={{0,96},{1,97},{2,98},{3,99},{4,7},{5,4},{6,5},{7,6},{8,104},{9,105... | collective-permute-start | bytes 2359304 | tf_op jit(solution)/shard_map/ppermute | solution.py:41
  182.5 30.6 %collective-permute-start.43 = (bf16[64,1536]{1,0:T(8,128)(2,1)S(1)}, bf16[64,1536]{1,0:T(8,128)(2,1)S(1)}, u32[]{:S(2)}, u32[]{:S(2)}) collective-permute-start(bf16[64,1536]{1,0:T(8,128)(2,1)S(1)} %get-tuple-element.34), channel_id=1, source_target_pairs={{0,1},{1,2},{2,3},{3,0},{4,36},{5,37},{6,38},{7,39},{8,9},{9,10},{... | collective-permute-start | bytes 589832 | tf_op jit(solution)/shard_map/ppermute | solution.py:41
  183.7 30.3 %collective-permute-start.44 = (bf16[64,1536]{1,0:T(8,128)(2,1)S(1)}, bf16[64,1536]{1,0:T(8,128)(2,1)S(1)}, u32[]{:S(2)}, u32[]{:S(2)}) collective-permute-start(bf16[64,1536]{1,0:T(8,128)(2,1)S(1)} %get-tuple-element.36), channel_id=1, source_target_pairs={{0,2},{1,3},{2,0},{3,1},{4,68},{5,69},{6,70},{7,71},{8,10},{9,11},... | collective-permute-start | bytes 589832 | tf_op jit(solution)/shard_map/ppermute | solution.py:41
  192.0 21.9 %collective-permute-start.45 = (bf16[64,1536]{1,0:T(8,128)(2,1)S(1)}, bf16[64,1536]{1,0:T(8,128)(2,1)S(1)}, u32[]{:S(2)}, u32[]{:S(2)}) collective-permute-start(bf16[64,1536]{1,0:T(8,128)(2,1)S(1)} %get-tuple-element.35), channel_id=1, source_target_pairs={{0,3},{1,0},{2,1},{3,2},{4,100},{5,101},{6,102},{7,103},{8,11},{9,... | collective-permute-start | bytes 589832 | tf_op jit(solution)/shard_map/ppermute | solution.py:41
  (27 other events, 459.2 us)

commit v2 on v0

v2 whole, which is shorter than its diff:
```python
import functools

import jax
import jax.numpy as jnp
from jax import lax
from jax.experimental import pallas as pl
from jax.experimental.pallas import tpu as pltpu
from jax.sharding import PartitionSpec as P

curve = 0.7978845608028654
cubic = 0.044715
AXES = ("depth", "row", "col")
BLOCK = 64
LIGHT = pl.CostEstimate(flops=1, bytes_accessed=1, transcendentals=0)


def gelu_value(value):
    tangent = jnp.tanh(curve * (value + cubic * value * value * value))
    return 0.5 * value * (1.0 + tangent)


def gelu_slope(value):
    tangent = jnp.tanh(curve * (value + cubic * value * value * value))
    return 0.5 * (1.0 + tangent) + 0.5 * value * (1.0 - tangent * tangent) * curve * (
        1.0 + 3.0 * cubic * value * value
    )


def device_pairs(move):
    pairs = []
    for z in range(4):
        for r in range(8):
            for x in range(4):
                to_z, to_y, to_core, to_x = move(z, r // 2, r % 2, x)
                source = z * 32 + r * 4 + x
                target = (to_z % 4) * 32 + ((to_y % 4) * 2 + to_core) * 4 + to_x % 4
                pairs.append((source, target))
    return pairs


def send(value, move):
    return lax.ppermute(value, AXES, device_pairs(move))


def first_axis(k):
    return lambda z, y, core, x: (z + k * core, y, core, x + k * (1 - core))


def second_axis(k):
    return lambda z, y, core, x: (z + k * (1 - core), y, core, x + k * core)


def along_y(z, y, core, x):
    return (z, y + 1 - 2 * core, core, x)


def other_core(z, y, core, x):
    return (z, y, 1 - core, x)


def place_term(dz, dx, core, y):
    slot = lax.rem(dx - y + 4, 4)
    low = lax.div(dz, 2)
    owner = jnp.where(slot == 1, 0, jnp.where(slot == 3, 1, low))
    near = lax.rem(dz + 2 * owner, 4)
    index = jnp.where(lax.rem(slot, 2) == 1, near, 6 - slot + lax.rem(dz, 2))
    return jnp.where(owner == core, 8, 0) + index


def gathered(group, block):
    def place(core, y, z, x):
        dz = jnp.where(core == 0, group, block)
        dx = jnp.where(core == 0, block, group)
        return place_term(dz, dx, core, y)

    return place


def summed(dz, dx, core):
    return jnp.where(core == 0, dz * 4 + dx, dx * 4 + dz)


def own_rows(block):
    return lambda core, y, z, x: summed(lax.rem(block + 2 * core, 4), y, core)


def near_rows(block, other):
    def place(core, y, z, x):
        holder = 1 - core if other else core
        return summed(lax.rem(block + 2 * holder, 4), lax.rem(y + 3 + 2 * holder, 4), core)

    return place


def far_rows(block, other):
    def place(core, y, z, x):
        holder = 1 - core if other else core
        return summed(block + 2 * holder, lax.rem(y + 2, 4), core)

    return place


def load_kernel(source, out, arrived):
    copy = pltpu.make_async_copy(source, out, arrived)
    copy.start()
    copy.wait()


def load(value):
    return pl.pallas_call(
        load_kernel,
        out_shape=jax.ShapeDtypeStruct(value.shape, value.dtype),
        in_specs=[pl.BlockSpec(memory_space=pltpu.HBM)],
        out_specs=pl.BlockSpec(memory_space=pltpu.VMEM),
        scratch_shapes=[pltpu.SemaphoreType.DMA],
        compiler_params=pltpu.CompilerParams(vmem_limit_bytes=16 * 2**20),
        cost_estimate=LIGHT,
    )(value)


def matmul_kernel(transposed, places, formed_places, *refs):
    sources, weight = refs[: len(places)], refs[len(places)]
    formed, out = refs[len(places) + 1 : -1], refs[-1]
    row = lax.axis_index("row")
    where = (lax.rem(row, 2), lax.div(row, 2), lax.axis_index("depth"), lax.axis_index("col"))
    contract = 1 if transposed else 0

    def put(value, blocks):
        for n, place in enumerate(blocks):
            at = place if isinstance(place, int) else place(*where)
            out[pl.ds(pl.multiple_of(at * BLOCK, BLOCK), BLOCK)] = value[n * BLOCK : (n + 1) * BLOCK]

    def multiply(left, blocks):
        product = lax.dot_general(
            left,
            weight[...],
            (((1,), (contract,)), ((), ())),
            preferred_element_type=jnp.float32,
        ).astype(jnp.bfloat16)
        put(product, blocks)

    small, small_blocks = [], []
    for source, blocks in zip(sources, places):
        if len(blocks) < 4:
            small.append(source[...])
            small_blocks += blocks
        else:
            for first in range(0, len(blocks), 4):
                rows = slice(first * BLOCK, (first + 4) * BLOCK)
                multiply(source[rows], blocks[first : first + 4])
    if small:
        multiply(jnp.concatenate(small), small_blocks)
    for source, blocks in zip(formed, formed_places):
        for n in range(len(blocks)):
            put(source[n * BLOCK : (n + 1) * BLOCK], blocks[n : n + 1])


def matmul(sources, places, weight, transposed, formed=(), formed_places=()):
    depth = weight.shape[1] if transposed else weight.shape[0]
    width = weight.shape[0] if transposed else weight.shape[1]
    total = sum(source.shape[0] for source in sources)
    rows = total + sum(value.shape[0] for value in formed)
    return pl.pallas_call(
        functools.partial(matmul_kernel, transposed, places, formed_places),
        out_shape=jax.ShapeDtypeStruct((rows, width), jnp.bfloat16),
        in_specs=[pl.BlockSpec(memory_space=pltpu.VMEM)] * (len(sources) + 1 + len(formed)),
        out_specs=pl.BlockSpec(memory_space=pltpu.VMEM),
        compiler_params=pltpu.CompilerParams(vmem_limit_bytes=24 * 2**20),
        cost_estimate=LIGHT,
    )(*sources, weight, *formed)


def in_order(count):
    return list(range(count))


def after(value, *others):
    return lax.optimization_barrier((value, *others))[0]


def sum_parts(*parts):
    total = parts[0].astype(jnp.float32)
    for part in parts[1:]:
        total = total + part.astype(jnp.float32)
    return total


def rounded(*parts):
    return sum_parts(*parts).astype(jnp.bfloat16)


def cut(value, parts):
    size = value.shape[0] // parts
    return [value[k * size : (k + 1) * size] for k in range(parts)]


def gather_line(own):
    return jnp.concatenate([own] + [send(own, first_axis(-k)) for k in (1, 2, 3)])


def gather_tokens(line, weight, transposed):
    up, down = send(line, second_axis(-1)), send(line, second_axis(1))
    rest = [send(up[:128], second_axis(-1)), send(down[128:], second_axis(1))]
    early = matmul(
        [line, up, down], [in_order(4), [4, 5, 6, 7], [8, 9, 10, 11]], weight, transposed
    )
    late_places = [[gathered(2, n) for n in range(2)], [gathered(2, n) for n in range(2, 4)]]
    early_places = [gathered(k, n) for k in (0, 1, 3) for n in range(4)]
    return matmul(rest, late_places, weight, transposed, [early], [early_places]), up, down


def reduce_rows(terms):
    both = rounded(terms[512:], send(terms[:512], other_core))
    far = send(both[256:384], along_y)
    near = jnp.concatenate([rounded(both[:128], far), both[128:256]])
    arrived = send(near, along_y)
    mine = jnp.concatenate([rounded(arrived[:128], both[384:]), arrived[128:]])
    other = send(mine, other_core)
    return sum_parts(mine, jnp.concatenate([other[128:], other[:128]]))


def gather_rows(own, weight, transposed):
    near = send(own, along_y)
    far = send(near[:128], along_y)
    other_near = send(near, other_core)
    early = matmul([own, near], [in_order(4), [4, 5, 6, 7]], weight, transposed)
    other_far = send(far, other_core)
    return matmul(
        [other_near, far, other_far],
        [
            [near_rows(n, True) for n in range(4)],
            [far_rows(n, False) for n in range(2)],
            [far_rows(n, True) for n in range(2)],
        ],
        weight,
        transposed,
        [early],
        [[own_rows(n) for n in range(4)] + [near_rows(n, False) for n in range(4)]],
    )


def reduce_tokens(terms):
    parts = cut(terms, 4)
    up, down = send(parts[2][:128], second_axis(1)), send(parts[2][128:], second_axis(-1))
    one = jnp.concatenate([rounded(parts[1][:128], up), parts[1][128:]])
    three = jnp.concatenate([parts[3][:128], rounded(parts[3][128:], down)])
    line = rounded(parts[0], send(one, second_axis(1)), send(three, second_axis(-1)))
    blocks = cut(line, 4)
    return rounded(blocks[0], *[send(blocks[k], first_axis(k)) for k in (1, 2, 3)])


def shards(inputs, w_in, w_out, out_grad):
    line = gather_line(inputs)
    w_in = load(after(w_in, line))
    terms, up, down = gather_tokens(line, w_in, False)
    grad_line = gather_line(after(out_grad, line))
    w_out = load(after(w_out, w_in))
    grad_terms, _, _ = gather_tokens(after(grad_line, up, down), w_out, True)
    pre = reduce_rows(terms)
    grad_act = reduce_rows(grad_terms)
    act = gelu_value(pre).astype(jnp.bfloat16)
    grad_pre = (grad_act * gelu_slope(pre)).astype(jnp.bfloat16)
    outputs = reduce_tokens(gather_rows(act, w_out, False))
    in_grad = reduce_tokens(gather_rows(grad_pre, w_in, True))
    return (outputs, in_grad)


def solution(mesh):
    in_specs = (
        P(("depth", "col"), "row"),
        P("row", ("depth", "col")),
        P(("depth", "col"), "row"),
        P(("depth", "col"), "row"),
    )
    out_specs = (P(("depth", "col"), "row"), P(("depth", "col"), "row"))
    return jax.shard_map(shards, mesh=mesh, in_specs=in_specs, out_specs=out_specs, check_vma=False)
```

time: 436 us -> 179 us (0.41)
  waiting for transfers between devices: 376 us -> 94.4 us
  starting transfers between devices: 0.32 us -> 51.4 us
  matrix products: 38.9 us -> 0 us
  Pallas kernels: 0 us -> 22.4 us
  between operations: 14.1 us -> 1.21 us
    reduce_scatter x4 -> x0, waiting for transfers between devices: 236 us -> none  [the longest x1 82.4 us: shards(): lax.psum_scatter(input_terms, ('depth', 'col'), scatter_dimension=0, tile...]
    all_gather x4 -> x0, waiting for transfers between devices: 138 us -> none  [the longest x1 52 us: shards(): lax.all_gather(inputs, ('depth', 'col'), axis=0, tiled=True)]
    ppermute x0 -> x44, waiting for transfers between devices: none -> 94.4 us  [send(): return lax.ppermute(value, AXES, device_pairs(move))]
    ppermute x0 -> x44, starting transfers between devices: none -> 51.4 us  [send(): return lax.ppermute(value, AXES, device_pairs(move))]
    dot_general x4 -> x0, matrix products: 38.9 us -> none  [the longest x2 19.5 us: transposed(): lax.dot_general(left, right, (((1,), (1,)), ((), ())), preferred_element_...]
    pallas_call x0 -> x10, Pallas kernels: none -> 22.4 us  [the longest x8 21.7 us: matmul(): pl.pallas_call(functools.partial(matmul_kernel, transposed, places, forme...]
  transfers between devices with their start and end apart: 8 -> 44, of which waited for: 8 -> 22; matrix products, arithmetic and copies ran while one was open for 9% -> 3% of each run, Pallas kernels for 0% -> 12%
where the time goes in v2:
time: 179 us
  waiting for transfers between devices  94.4 us (53%)
  starting transfers between devices  51.4 us (29%)
  Pallas kernels  22.4 us (13%)
  other arithmetic  5.66 us (3%)
  local copies, waits for them, and re-layouts  4.29 us (2%)
    ppermute x44, waiting for transfers between devices, send(): return lax.ppermute(value, AXES, device_pairs(move))  94.4 us
    ppermute x44, starting transfers between devices, send(): return lax.ppermute(value, AXES, device_pairs(move))  51.4 us
    pallas_call x8, Pallas kernels, matmul(): pl.pallas_call(functools.partial(matmul_kernel, transposed, places, forme...  21.7 us
    convert_element_type x12, other arithmetic, rounded(): return sum_parts(*parts).astype(jnp.bfloat16)  3.73 us
  transfers between devices with their start and end apart: 44, of which 22 were waited for; matrix products, arithmetic and copies ran while one was open for 3% of the time, Pallas kernels for 12%

profile of v2, /device:TPU:0, one launch (start us, length us, event | category | flops | bytes accessed | tf_op | source)
XLA Modules:
  0.0 179.3 jit_solution(655605530912052411)
XLA Ops:
  0.6 3.2 %collective-permute-start.1 = (bf16[64,1536]{1,0:T(8,128)(2,1)}, bf16[64,1536]{1,0:T(8,128)(2,1)S(1)}, u32[]{:S(2)}, u32[]{:S(2)}) collective-permute-start(bf16[64,1536]{1,0:T(8,128)(2,1)} %param.4), channel_id=1, source_target_pairs={{0,2},{1,3},{2,0},{3,1},{4,68},{5,69},{6,70},{7,71},{8,10},{9,11},... | collective-permute-start | bytes 589832 | tf_op jit(solution)/shard_map/ppermute | solution.py:42
  6.8 3.5 %collective-permute-done = bf16[64,1536]{1,0:T(8,128)(2,1)S(1)} collective-permute-done((bf16[64,1536]{1,0:T(8,128)(2,1)}, bf16[64,1536]{1,0:T(8,128)(2,1)S(1)}, u32[]{:S(2)}, u32[]{:S(2)}) %collective-permute-start) | collective-permute-done | bytes 196640 | tf_op jit(solution)/shard_map/ppermute | solution.py:42
  20.2 10.0 %collective-permute-done.5.refs_2_ = bf16[256,1536]{1,0:T(8,128)(2,1)S(1)} collective-permute-done((bf16[256,1536]{1,0:T(8,128)(2,1)S(1)}, bf16[256,1536]{1,0:T(8,128)(2,1)S(1)}, u32[]{:S(2)}, u32[]{:S(2)}) %collective-permute-start.5) | collective-permute-done | bytes 786464 | tf_op jit(solution)/shard_map/ppermute | solution.py:42
  30.3 3.3 %collective-permute-start.4 = (bf16[128,1536]{1,0:T(8,128)(2,1)S(1)}, bf16[128,1536]{1,0:T(8,128)(2,1)S(1)}, u32[]{:S(2)}, u32[]{:S(2)}) collective-permute-start(bf16[128,1536]{1,0:T(8,128)(2,1)S(1)} %slice.210), channel_id=1, source_target_pairs={{0,96},{1,97},{2,98},{3,99},{4,7},{5,4},{6,5},{7,6},{8,104},{9,105... | collective-permute-start | bytes 1179656 | tf_op jit(solution)/shard_map/ppermute | solution.py:42
  33.7 3.2 %collective-permute-start.25 = (bf16[256,1536]{1,0:T(8,128)(2,1)S(1)}, bf16[256,1536]{1,0:T(8,128)(2,1)S(1)}, u32[]{:S(2)}, u32[]{:S(2)}) collective-permute-start(bf16[256,1536]{1,0:T(8,128)(2,1)S(1)} %pad_maximum_fusion.5.refs_0_), channel_id=1, source_target_pairs={{0,96},{1,97},{2,98},{3,99},{4,7},{5,4},{6,5},{7,6},{8,104},{9,105... | collective-permute-start | bytes 2359304 | tf_op jit(solution)/shard_map/ppermute | solution.py:42
  39.6 3.8 %shard_map.60.refs_3_ = bf16[768,1536]{1,0:T(8,128)(2,1)S(1)} custom-call(bf16[256,1536]{1,0:T(8,128)(2,1)S(1)} %constant_dynamic-update-slice_fusion.refs_0_, bf16[256,1536]{1,0:T(8,128)(2,1)S(1)} %collective-permute-done.3.refs_1_, bf16[256,1536]{1,0:T(8,128)(2,1)S(1)} %collective-permute-done.5.refs_2_, bf16[1536,1536]{1,0:T(8,128)(2,1)S(1)} %shard_map.59.refs_3_.refs_2_), custom_call_target="tpu_custom_call" | custom-call | flops 1 | bytes 1 | tf_op jit(solution)/shard_map/pallas_call | solution.py:163
  47.8 3.5 %collective-permute-start.26 = (bf16[128,1536]{1,0:T(8,128)(2,1)S(1)}, bf16[128,1536]{1,0:T(8,128)(2,1)S(1)}, u32[]{:S(2)}, u32[]{:S(2)}) collective-permute-start(bf16[128,1536]{1,0:T(8,128)(2,1)S(1)} %slice.234), channel_id=1, source_target_pairs={{0,96},{1,97},{2,98},{3,99},{4,7},{5,4},{6,5},{7,6},{8,104},{9,105... | collective-permute-start | bytes 1179656 | tf_op jit(solution)/shard_map/ppermute | solution.py:42
  51.6 3.8 %shard_map.65.refs_3_ = bf16[768,1536]{1,0:T(8,128)(2,1)S(1)} custom-call(bf16[256,1536]{1,0:T(8,128)(2,1)S(1)} %pad_maximum_fusion.5.refs_0_, bf16[256,1536]{1,0:T(8,128)(2,1)S(1)} %collective-permute-done.25.refs_1_, bf16[256,1536]{1,0:T(8,128)(2,1)S(1)} %collective-permute-done.27.refs_2_, bf16[1536,1536]{1,0:T(8,128)(2,1)S(1)} %shard_map.62.refs_2_.refs_3_), custom_call_target="tpu_custom_call" | custom-call | flops 1 | bytes 1 | tf_op jit(solution)/shard_map/pallas_call | solution.py:163
  64.1 4.0 %collective-permute-done.8 = bf16[128,1536]{1,0:T(8,128)(2,1)S(1)} collective-permute-done((bf16[128,1536]{1,0:T(8,128)(2,1)S(1)}, bf16[128,1536]{1,0:T(8,128)(2,1)S(1)}, u32[]{:S(2)}, u32[]{:S(2)}) %collective-permute-start.8) | collective-permute-done | bytes 393248 | tf_op jit(solution)/shard_map/ppermute | solution.py:42
  68.7 3.6 %collective-permute-done.30 = bf16[128,1536]{1,0:T(8,128)(2,1)S(1)} collective-permute-done((bf16[128,1536]{1,0:T(8,128)(2,1)S(1)}, bf16[128,1536]{1,0:T(8,128)(2,1)S(1)}, u32[]{:S(2)}, u32[]{:S(2)}) %collective-permute-start.30) | collective-permute-done | bytes 393248 | tf_op jit(solution)/shard_map/ppermute | solution.py:42
  72.9 8.6 %collective-permute-done.9 = bf16[256,1536]{1,0:T(8,128)(2,1)S(1)} collective-permute-done((bf16[256,1536]{1,0:T(8,128)(2,1)S(1)}, bf16[256,1536]{1,0:T(8,128)(2,1)S(1)}, u32[]{:S(2)}, u32[]{:S(2)}) %collective-permute-start.9) | collective-permute-done | bytes 786464 | tf_op jit(solution)/shard_map/ppermute | solution.py:42
  81.8 8.1 %collective-permute-done.31 = bf16[256,1536]{1,0:T(8,128)(2,1)S(1)} collective-permute-done((bf16[256,1536]{1,0:T(8,128)(2,1)S(1)}, bf16[256,1536]{1,0:T(8,128)(2,1)S(1)}, u32[]{:S(2)}, u32[]{:S(2)}) %collective-permute-start.31) | collective-permute-done | bytes 786464 | tf_op jit(solution)/shard_map/ppermute | solution.py:42
  95.3 12.0 %collective-permute-done.11.refs_1_ = bf16[256,1536]{1,0:T(8,128)(2,1)S(1)} collective-permute-done((bf16[256,1536]{1,0:T(8,128)(2,1)S(1)}, bf16[256,1536]{1,0:T(8,128)(2,1)S(1)}, u32[]{:S(2)}, u32[]{:S(2)}) %collective-permute-start.11) | collective-permute-done | bytes 786464 | tf_op jit(solution)/shard_map/ppermute | solution.py:42
  107.5 8.2 %collective-permute-done.33.refs_1_ = bf16[256,1536]{1,0:T(8,128)(2,1)S(1)} collective-permute-done((bf16[256,1536]{1,0:T(8,128)(2,1)S(1)}, bf16[256,1536]{1,0:T(8,128)(2,1)S(1)}, u32[]{:S(2)}, u32[]{:S(2)}) %collective-permute-start.33) | collective-permute-done | bytes 786464 | tf_op jit(solution)/shard_map/ppermute | solution.py:42
  115.8 4.1 %collective-permute-done.13.refs_1_ = bf16[128,1536]{1,0:T(8,128)(2,1)S(1)} collective-permute-done((bf16[128,1536]{1,0:T(8,128)(2,1)S(1)}, bf16[128,1536]{1,0:T(8,128)(2,1)S(1)}, u32[]{:S(2)}, u32[]{:S(2)}) %collective-permute-start.13) | collective-permute-done | bytes 393248 | tf_op jit(solution)/shard_map/ppermute | solution.py:42
  128.8 3.6 %collective-permute-start.17 = (bf16[128,1536]{1,0:T(8,128)(2,1)S(1)}, bf16[128,1536]{1,0:T(8,128)(2,1)S(1)}, u32[]{:S(2)}, u32[]{:S(2)}) collective-permute-start(bf16[128,1536]{1,0:T(8,128)(2,1)S(1)} %get-tuple-element.19), channel_id=1, source_target_pairs={{0,96},{1,97},{2,98},{3,99},{4,7},{5,4},{6,5},{7,6},{8,104},{9,105... | collective-permute-start | bytes 1179656 | tf_op jit(solution)/shard_map/ppermute | solution.py:42
  132.4 2.8 %shard_map.68 = bf16[1024,1536]{1,0:T(8,128)(2,1)S(1)} custom-call(bf16[256,1536]{1,0:T(8,128)(2,1)S(1)} %collective-permute-done.34.refs_0_, bf16[128,1536]{1,0:T(8,128)(2,1)S(1)} %collective-permute-done.35.refs_1_, bf16[128,1536]{1,0:T(8,128)(2,1)S(1)} %collective-permute-done.36.refs_2_, bf16[1536,1536]{1,0:T(8,128)(2,1)S(1)} %shard_map.59.refs_3_.refs_2_, ...), custom_call_target="tpu_custom_call" | custom-call | flops 1 | bytes 1 | tf_op jit(solution)/shard_map/pallas_call | solution.py:163
  135.4 3.2 %collective-permute-start.39 = (bf16[128,1536]{1,0:T(8,128)(2,1)S(1)}, bf16[128,1536]{1,0:T(8,128)(2,1)S(1)}, u32[]{:S(2)}, u32[]{:S(2)}) collective-permute-start(bf16[128,1536]{1,0:T(8,128)(2,1)S(1)} %get-tuple-element.13), channel_id=1, source_target_pairs={{0,96},{1,97},{2,98},{3,99},{4,7},{5,4},{6,5},{7,6},{8,104},{9,105... | collective-permute-start | bytes 1179656 | tf_op jit(solution)/shard_map/ppermute | solution.py:42
  138.9 2.8 %collective-permute-start.18 = (bf16[256,1536]{1,0:T(8,128)(2,1)S(1)}, bf16[256,1536]{1,0:T(8,128)(2,1)S(1)}, u32[]{:S(2)}, u32[]{:S(2)}) collective-permute-start(bf16[256,1536]{1,0:T(8,128)(2,1)S(1)} %pad_maximum_fusion.4), channel_id=1, source_target_pairs={{0,96},{1,97},{2,98},{3,99},{4,7},{5,4},{6,5},{7,6},{8,104},{9,105... | collective-permute-start | bytes 2359304 | tf_op jit(solution)/shard_map/ppermute | solution.py:42
  144.7 3.3 %collective-permute-start.40 = (bf16[256,1536]{1,0:T(8,128)(2,1)S(1)}, bf16[256,1536]{1,0:T(8,128)(2,1)S(1)}, u32[]{:S(2)}, u32[]{:S(2)}) collective-permute-start(bf16[256,1536]{1,0:T(8,128)(2,1)S(1)} %pad_maximum_fusion.9), channel_id=1, source_target_pairs={{0,96},{1,97},{2,98},{3,99},{4,7},{5,4},{6,5},{7,6},{8,104},{9,105... | collective-permute-start | bytes 2359304 | tf_op jit(solution)/shard_map/ppermute | solution.py:42
  148.1 4.3 %collective-permute-done.18 = bf16[256,1536]{1,0:T(8,128)(2,1)S(1)} collective-permute-done((bf16[256,1536]{1,0:T(8,128)(2,1)S(1)}, bf16[256,1536]{1,0:T(8,128)(2,1)S(1)}, u32[]{:S(2)}, u32[]{:S(2)}) %collective-permute-start.18) | collective-permute-done | bytes 786464 | tf_op jit(solution)/shard_map/ppermute | solution.py:42
  155.5 3.2 %collective-permute-start.21 = (bf16[64,1536]{1,0:T(8,128)(2,1)S(1)}, bf16[64,1536]{1,0:T(8,128)(2,1)S(1)}, u32[]{:S(2)}, u32[]{:S(2)}) collective-permute-start(bf16[64,1536]{1,0:T(8,128)(2,1)S(1)} %get-tuple-element.34), channel_id=1, source_target_pairs={{0,3},{1,0},{2,1},{3,2},{4,100},{5,101},{6,102},{7,103},{8,11},{9,... | collective-permute-start | bytes 589832 | tf_op jit(solution)/shard_map/ppermute | solution.py:42
  159.0 6.0 %collective-permute-done.40 = bf16[256,1536]{1,0:T(8,128)(2,1)S(1)} collective-permute-done((bf16[256,1536]{1,0:T(8,128)(2,1)S(1)}, bf16[256,1536]{1,0:T(8,128)(2,1)S(1)}, u32[]{:S(2)}, u32[]{:S(2)}) %collective-permute-start.40) | collective-permute-done | bytes 786464 | tf_op jit(solution)/shard_map/ppermute | solution.py:42
  168.1 3.2 %collective-permute-start.43 = (bf16[64,1536]{1,0:T(8,128)(2,1)S(1)}, bf16[64,1536]{1,0:T(8,128)(2,1)S(1)}, u32[]{:S(2)}, u32[]{:S(2)}) collective-permute-start(bf16[64,1536]{1,0:T(8,128)(2,1)S(1)} %get-tuple-element.29), channel_id=1, source_target_pairs={{0,3},{1,0},{2,1},{3,2},{4,100},{5,101},{6,102},{7,103},{8,11},{9,... | collective-permute-start | bytes 589832 | tf_op jit(solution)/shard_map/ppermute | solution.py:42
  (127 shorter events, 62.5 us)
Async XLA Ops:
  12.1 18.0 %collective-permute-start.5 = (bf16[256,1536]{1,0:T(8,128)(2,1)S(1)}, bf16[256,1536]{1,0:T(8,128)(2,1)S(1)}, u32[]{:S(2)}, u32[]{:S(2)}) collective-permute-start(bf16[256,1536]{1,0:T(8,128)(2,1)S(1)} %constant_dynamic-update-slice_fusion.refs_0_), channel_id=1, source_target_pairs={{0,32},{1,33},{2,34},{3,35},{4,5},{5,6},{6,7},{7,4},{8,40},{9,41},... | collective-permute-start | bytes 2359304 | tf_op jit(solution)/shard_map/ppermute | solution.py:42
  14.1 16.2 %collective-permute-start.3 = (bf16[256,1536]{1,0:T(8,128)(2,1)S(1)}, bf16[256,1536]{1,0:T(8,128)(2,1)S(1)}, u32[]{:S(2)}, u32[]{:S(2)}) collective-permute-start(bf16[256,1536]{1,0:T(8,128)(2,1)S(1)} %constant_dynamic-update-slice_fusion.refs_0_), channel_id=1, source_target_pairs={{0,96},{1,97},{2,98},{3,99},{4,7},{5,4},{6,5},{7,6},{8,104},{9,105... | collective-permute-start | bytes 2359304 | tf_op jit(solution)/shard_map/ppermute | solution.py:42
  16.3 17.3 %collective-permute-start.24 = (bf16[64,1536]{1,0:T(8,128)(2,1)S(1)}, bf16[64,1536]{1,0:T(8,128)(2,1)S(1)}, u32[]{:S(2)}, u32[]{:S(2)}) collective-permute-start(bf16[64,1536]{1,0:T(8,128)(2,1)S(1)} %copy-done.1), channel_id=1, source_target_pairs={{0,1},{1,2},{2,3},{3,0},{4,36},{5,37},{6,38},{7,39},{8,9},{9,10},{... | collective-permute-start | bytes 589832 | tf_op jit(solution)/shard_map/ppermute | solution.py:42
  16.3 17.3 %collective-permute-start.23 = (bf16[64,1536]{1,0:T(8,128)(2,1)S(1)}, bf16[64,1536]{1,0:T(8,128)(2,1)S(1)}, u32[]{:S(2)}, u32[]{:S(2)}) collective-permute-start(bf16[64,1536]{1,0:T(8,128)(2,1)S(1)} %copy-done.1), channel_id=1, source_target_pairs={{0,2},{1,3},{2,0},{3,1},{4,68},{5,69},{6,70},{7,71},{8,10},{9,11},... | collective-permute-start | bytes 589832 | tf_op jit(solution)/shard_map/ppermute | solution.py:42
  18.8 14.8 %collective-permute-start.22 = (bf16[64,1536]{1,0:T(8,128)(2,1)S(1)}, bf16[64,1536]{1,0:T(8,128)(2,1)S(1)}, u32[]{:S(2)}, u32[]{:S(2)}) collective-permute-start(bf16[64,1536]{1,0:T(8,128)(2,1)S(1)} %copy-done.1), channel_id=1, source_target_pairs={{0,3},{1,0},{2,1},{3,2},{4,100},{5,101},{6,102},{7,103},{8,11},{9,... | collective-permute-start | bytes 589832 | tf_op jit(solution)/shard_map/ppermute | solution.py:42
  30.1 13.3 %collective-permute-start.6 = (bf16[128,1536]{1,0:T(8,128)(2,1)S(1)}, bf16[128,1536]{1,0:T(8,128)(2,1)S(1)}, u32[]{:S(2)}, u32[]{:S(2)}) collective-permute-start(bf16[128,1536]{1,0:T(8,128)(2,1)S(1)} %slice.211), channel_id=1, source_target_pairs={{0,32},{1,33},{2,34},{3,35},{4,5},{5,6},{6,7},{7,4},{8,40},{9,41},... | collective-permute-start | bytes 1179656 | tf_op jit(solution)/shard_map/ppermute | solution.py:42
  30.3 13.2 %collective-permute-start.4 = (bf16[128,1536]{1,0:T(8,128)(2,1)S(1)}, bf16[128,1536]{1,0:T(8,128)(2,1)S(1)}, u32[]{:S(2)}, u32[]{:S(2)}) collective-permute-start(bf16[128,1536]{1,0:T(8,128)(2,1)S(1)} %slice.210), channel_id=1, source_target_pairs={{0,96},{1,97},{2,98},{3,99},{4,7},{5,4},{6,5},{7,6},{8,104},{9,105... | collective-permute-start | bytes 1179656 | tf_op jit(solution)/shard_map/ppermute | solution.py:42
  33.7 14.0 %collective-permute-start.27 = (bf16[256,1536]{1,0:T(8,128)(2,1)S(1)}, bf16[256,1536]{1,0:T(8,128)(2,1)S(1)}, u32[]{:S(2)}, u32[]{:S(2)}) collective-permute-start(bf16[256,1536]{1,0:T(8,128)(2,1)S(1)} %pad_maximum_fusion.5.refs_0_), channel_id=1, source_target_pairs={{0,32},{1,33},{2,34},{3,35},{4,5},{5,6},{6,7},{7,4},{8,40},{9,41},... | collective-permute-start | bytes 2359304 | tf_op jit(solution)/shard_map/ppermute | solution.py:42
  33.7 14.0 %collective-permute-start.25 = (bf16[256,1536]{1,0:T(8,128)(2,1)S(1)}, bf16[256,1536]{1,0:T(8,128)(2,1)S(1)}, u32[]{:S(2)}, u32[]{:S(2)}) collective-permute-start(bf16[256,1536]{1,0:T(8,128)(2,1)S(1)} %pad_maximum_fusion.5.refs_0_), channel_id=1, source_target_pairs={{0,96},{1,97},{2,98},{3,99},{4,7},{5,4},{6,5},{7,6},{8,104},{9,105... | collective-permute-start | bytes 2359304 | tf_op jit(solution)/shard_map/ppermute | solution.py:42
  45.2 13.3 %collective-permute-start.7 = (bf16[512,1536]{1,0:T(8,128)(2,1)S(1)}, bf16[512,1536]{1,0:T(8,128)(2,1)S(1)}, u32[]{:S(2)}, u32[]{:S(2)}) collective-permute-start(bf16[512,1536]{1,0:T(8,128)(2,1)S(1)} %slice.213), channel_id=1, source_target_pairs={{0,4},{1,5},{2,6},{3,7},{4,0},{5,1},{6,2},{7,3},{8,12},{9,13},{10,... | collective-permute-start | bytes 4718600 | tf_op jit(solution)/shard_map/ppermute | solution.py:42
  68.3 13.3 %collective-permute-start.9 = (bf16[256,1536]{1,0:T(8,128)(2,1)S(1)}, bf16[256,1536]{1,0:T(8,128)(2,1)S(1)}, u32[]{:S(2)}, u32[]{:S(2)}) collective-permute-start(bf16[256,1536]{1,0:T(8,128)(2,1)S(1)} %pad_maximum_fusion), channel_id=1, source_target_pairs={{0,8},{1,9},{2,10},{3,11},{4,28},{5,29},{6,30},{7,31},{8,16},{9,17... | collective-permute-start | bytes 2359304 | tf_op jit(solution)/shard_map/ppermute | solution.py:42
  72.5 17.5 %collective-permute-start.31 = (bf16[256,1536]{1,0:T(8,128)(2,1)S(1)}, bf16[256,1536]{1,0:T(8,128)(2,1)S(1)}, u32[]{:S(2)}, u32[]{:S(2)}) collective-permute-start(bf16[256,1536]{1,0:T(8,128)(2,1)S(1)} %pad_maximum_fusion.6), channel_id=1, source_target_pairs={{0,8},{1,9},{2,10},{3,11},{4,28},{5,29},{6,30},{7,31},{8,16},{9,17... | collective-permute-start | bytes 2359304 | tf_op jit(solution)/shard_map/ppermute | solution.py:42
  94.0 13.3 %collective-permute-start.11 = (bf16[256,1536]{1,0:T(8,128)(2,1)S(1)}, bf16[256,1536]{1,0:T(8,128)(2,1)S(1)}, u32[]{:S(2)}, u32[]{:S(2)}) collective-permute-start(bf16[256,1536]{1,0:T(8,128)(2,1)S(1)} %get-tuple-element.23.refs_0_), channel_id=1, source_target_pairs={{0,8},{1,9},{2,10},{3,11},{4,28},{5,29},{6,30},{7,31},{8,16},{9,17... | collective-permute-start | bytes 2359304 | tf_op jit(solution)/shard_map/ppermute | solution.py:42
  94.1 21.6 %collective-permute-start.33 = (bf16[256,1536]{1,0:T(8,128)(2,1)S(1)}, bf16[256,1536]{1,0:T(8,128)(2,1)S(1)}, u32[]{:S(2)}, u32[]{:S(2)}) collective-permute-start(bf16[256,1536]{1,0:T(8,128)(2,1)S(1)} %get-tuple-element.22.refs_0_), channel_id=1, source_target_pairs={{0,8},{1,9},{2,10},{3,11},{4,28},{5,29},{6,30},{7,31},{8,16},{9,17... | collective-permute-start | bytes 2359304 | tf_op jit(solution)/shard_map/ppermute | solution.py:42
  107.3 12.6 %collective-permute-start.13 = (bf16[128,1536]{1,0:T(8,128)(2,1)S(1)}, bf16[128,1536]{1,0:T(8,128)(2,1)S(1)}, u32[]{:S(2)}, u32[]{:S(2)}) collective-permute-start(bf16[128,1536]{1,0:T(8,128)(2,1)S(1)} %slice.222), channel_id=1, source_target_pairs={{0,8},{1,9},{2,10},{3,11},{4,28},{5,29},{6,30},{7,31},{8,16},{9,17... | collective-permute-start | bytes 1179656 | tf_op jit(solution)/shard_map/ppermute | solution.py:42
  107.4 18.4 %collective-permute-start.12 = (bf16[256,1536]{1,0:T(8,128)(2,1)S(1)}, bf16[256,1536]{1,0:T(8,128)(2,1)S(1)}, u32[]{:S(2)}, u32[]{:S(2)}) collective-permute-start(bf16[256,1536]{1,0:T(8,128)(2,1)S(1)} %collective-permute-done.11.refs_1_), channel_id=1, source_target_pairs={{0,4},{1,5},{2,6},{3,7},{4,0},{5,1},{6,2},{7,3},{8,12},{9,13},{10,... | collective-permute-start | bytes 2359304 | tf_op jit(solution)/shard_map/ppermute | solution.py:42
  120.0 12.5 %collective-permute-start.34 = (bf16[256,1536]{1,0:T(8,128)(2,1)S(1)}, bf16[256,1536]{1,0:T(8,128)(2,1)S(1)}, u32[]{:S(2)}, u32[]{:S(2)}) collective-permute-start(bf16[256,1536]{1,0:T(8,128)(2,1)S(1)} %collective-permute-done.33.refs_1_), channel_id=1, source_target_pairs={{0,4},{1,5},{2,6},{3,7},{4,0},{5,1},{6,2},{7,3},{8,12},{9,13},{10,... | collective-permute-start | bytes 2359304 | tf_op jit(solution)/shard_map/ppermute | solution.py:42
  138.9 13.5 %collective-permute-start.18 = (bf16[256,1536]{1,0:T(8,128)(2,1)S(1)}, bf16[256,1536]{1,0:T(8,128)(2,1)S(1)}, u32[]{:S(2)}, u32[]{:S(2)}) collective-permute-start(bf16[256,1536]{1,0:T(8,128)(2,1)S(1)} %pad_maximum_fusion.4), channel_id=1, source_target_pairs={{0,96},{1,97},{2,98},{3,99},{4,7},{5,4},{6,5},{7,6},{8,104},{9,105... | collective-permute-start | bytes 2359304 | tf_op jit(solution)/shard_map/ppermute | solution.py:42
  141.8 13.3 %collective-permute-start.16 = (bf16[256,1536]{1,0:T(8,128)(2,1)S(1)}, bf16[256,1536]{1,0:T(8,128)(2,1)S(1)}, u32[]{:S(2)}, u32[]{:S(2)}) collective-permute-start(bf16[256,1536]{1,0:T(8,128)(2,1)S(1)} %pad_maximum_fusion.3), channel_id=1, source_target_pairs={{0,32},{1,33},{2,34},{3,35},{4,5},{5,6},{6,7},{7,4},{8,40},{9,41},... | collective-permute-start | bytes 2359304 | tf_op jit(solution)/shard_map/ppermute | solution.py:42
  144.7 20.4 %collective-permute-start.40 = (bf16[256,1536]{1,0:T(8,128)(2,1)S(1)}, bf16[256,1536]{1,0:T(8,128)(2,1)S(1)}, u32[]{:S(2)}, u32[]{:S(2)}) collective-permute-start(bf16[256,1536]{1,0:T(8,128)(2,1)S(1)} %pad_maximum_fusion.9), channel_id=1, source_target_pairs={{0,96},{1,97},{2,98},{3,99},{4,7},{5,4},{6,5},{7,6},{8,104},{9,105... | collective-permute-start | bytes 2359304 | tf_op jit(solution)/shard_map/ppermute | solution.py:42
  148.0 19.7 %collective-permute-start.38 = (bf16[256,1536]{1,0:T(8,128)(2,1)S(1)}, bf16[256,1536]{1,0:T(8,128)(2,1)S(1)}, u32[]{:S(2)}, u32[]{:S(2)}) collective-permute-start(bf16[256,1536]{1,0:T(8,128)(2,1)S(1)} %pad_maximum_fusion.8), channel_id=1, source_target_pairs={{0,32},{1,33},{2,34},{3,35},{4,5},{5,6},{6,7},{7,4},{8,40},{9,41},... | collective-permute-start | bytes 2359304 | tf_op jit(solution)/shard_map/ppermute | solution.py:42
  155.4 15.9 %collective-permute-start.19 = (bf16[64,1536]{1,0:T(8,128)(2,1)S(1)}, bf16[64,1536]{1,0:T(8,128)(2,1)S(1)}, u32[]{:S(2)}, u32[]{:S(2)}) collective-permute-start(bf16[64,1536]{1,0:T(8,128)(2,1)S(1)} %get-tuple-element.33), channel_id=1, source_target_pairs={{0,1},{1,2},{2,3},{3,0},{4,36},{5,37},{6,38},{7,39},{8,9},{9,10},{... | collective-permute-start | bytes 589832 | tf_op jit(solution)/shard_map/ppermute | solution.py:42
  155.5 17.0 %collective-permute-start.21 = (bf16[64,1536]{1,0:T(8,128)(2,1)S(1)}, bf16[64,1536]{1,0:T(8,128)(2,1)S(1)}, u32[]{:S(2)}, u32[]{:S(2)}) collective-permute-start(bf16[64,1536]{1,0:T(8,128)(2,1)S(1)} %get-tuple-element.34), channel_id=1, source_target_pairs={{0,3},{1,0},{2,1},{3,2},{4,100},{5,101},{6,102},{7,103},{8,11},{9,... | collective-permute-start | bytes 589832 | tf_op jit(solution)/shard_map/ppermute | solution.py:42
  158.7 13.8 %collective-permute-start.20 = (bf16[64,1536]{1,0:T(8,128)(2,1)S(1)}, bf16[64,1536]{1,0:T(8,128)(2,1)S(1)}, u32[]{:S(2)}, u32[]{:S(2)}) collective-permute-start(bf16[64,1536]{1,0:T(8,128)(2,1)S(1)} %get-tuple-element.35), channel_id=1, source_target_pairs={{0,2},{1,3},{2,0},{3,1},{4,68},{5,69},{6,70},{7,71},{8,10},{9,11},... | collective-permute-start | bytes 589832 | tf_op jit(solution)/shard_map/ppermute | solution.py:42
  (24 other events, 195.1 us)

commit v3 on v2

--- a/solution.py
+++ b/solution.py
@@ -194,37 +194,55 @@
     return [value[k * size : (k + 1) * size] for k in range(parts)]
 
 
-def gather_line(own):
-    return jnp.concatenate([own] + [send(own, first_axis(-k)) for k in (1, 2, 3)])
-
-
-def gather_tokens(line, weight, transposed):
-    up, down = send(line, second_axis(-1)), send(line, second_axis(1))
-    rest = [send(up[:128], second_axis(-1)), send(down[128:], second_axis(1))]
-    early = matmul(
-        [line, up, down], [in_order(4), [4, 5, 6, 7], [8, 9, 10, 11]], weight, transposed
-    )
-    late_places = [[gathered(2, n) for n in range(2)], [gathered(2, n) for n in range(2, 4)]]
-    early_places = [gathered(k, n) for k in (0, 1, 3) for n in range(4)]
-    return matmul(rest, late_places, weight, transposed, [early], [early_places]), up, down
-
-
-def reduce_rows(terms):
-    both = rounded(terms[512:], send(terms[:512], other_core))
-    far = send(both[256:384], along_y)
-    near = jnp.concatenate([rounded(both[:128], far), both[128:256]])
-    arrived = send(near, along_y)
-    mine = jnp.concatenate([rounded(arrived[:128], both[384:]), arrived[128:]])
-    other = send(mine, other_core)
+def swap(value):
+    if value.shape[0] < 512:
+        return send(value, other_core)
+    return jnp.concatenate([send(part, other_core) for part in cut(value, 2)])
+
+
+def gather_lines(own, grad_own):
+    both = jnp.concatenate([own, grad_own])
+    parts = [send(both, first_axis(-k)) for k in (1, 2, 3)]
+    line = jnp.concatenate([own] + [part[:BLOCK] for part in parts])
+    return line, jnp.concatenate([grad_own] + [part[BLOCK:] for part in parts])
+
+
+def ring(line):
+    return send(line, second_axis(-1)), send(line, second_axis(1))
+
+
+def ring_rest(up, down):
+    return [send(up[:128], second_axis(-1)), send(down[128:], second_axis(1))]
+
+
+def near_terms(line, up, down, weight, transposed):
+    places = [in_order(4), [4, 5, 6, 7], [8, 9, 10, 11]]
+    return matmul([line, up, down], places, weight, transposed)
+
+
+def all_terms(rest, near, weight, transposed):
+    rest_places = [[gathered(2, n) for n in range(2)], [gathered(2, n) for n in range(2, 4)]]
+    near_places = [gathered(k, n) for k in (0, 1, 3) for n in range(4)]
+    return matmul(rest, rest_places, weight, transposed, [near], [near_places])
+
+
+def add_far(both, far):
+    return jnp.concatenate([rounded(both[:128], far), both[128:256]])
+
+
+def add_own(arrived, both):
+    return jnp.concatenate([rounded(arrived[:128], both[384:]), arrived[128:]])
+
+
+def add_other(mine, other):
     return sum_parts(mine, jnp.concatenate([other[128:], other[:128]]))
 
 
-def gather_rows(own, weight, transposed):
-    near = send(own, along_y)
-    far = send(near[:128], along_y)
-    other_near = send(near, other_core)
-    early = matmul([own, near], [in_order(4), [4, 5, 6, 7]], weight, transposed)
-    other_far = send(far, other_core)
+def early_sums(own, near, weight, transposed):
+    return matmul([own, near], [in_order(4), [4, 5, 6, 7]], weight, transposed)
+
+
+def all_sums(other_near, far, other_far, early, weight, transposed):
     return matmul(
         [other_near, far, other_far],
         [
@@ -239,29 +257,70 @@
     )
 
 
-def reduce_tokens(terms):
-    parts = cut(terms, 4)
-    up, down = send(parts[2][:128], second_axis(1)), send(parts[2][128:], second_axis(-1))
+def pass_far(parts):
+    return send(parts[2][:128], second_axis(1)), send(parts[2][128:], second_axis(-1))
+
+
+def pass_near(parts, up, down):
     one = jnp.concatenate([rounded(parts[1][:128], up), parts[1][128:]])
     three = jnp.concatenate([parts[3][:128], rounded(parts[3][128:], down)])
-    line = rounded(parts[0], send(one, second_axis(1)), send(three, second_axis(-1)))
+    return send(one, second_axis(1)), send(three, second_axis(-1))
+
+
+def finish(line):
     blocks = cut(line, 4)
     return rounded(blocks[0], *[send(blocks[k], first_axis(k)) for k in (1, 2, 3)])
 
 
 def shards(inputs, w_in, w_out, out_grad):
-    line = gather_line(inputs)
+    line, grad_line = gather_lines(inputs, out_grad)
+    up, down = ring(line)
     w_in = load(after(w_in, line))
-    terms, up, down = gather_tokens(line, w_in, False)
-    grad_line = gather_line(after(out_grad, line))
+    rest = ring_rest(after(up, w_in), after(down, w_in))
+    grad_up, grad_down = ring(grad_line)
+    near = near_terms(line, up, down, w_in, False)
+    grad_up, grad_down = after(grad_up, near), after(grad_down, near)
+    terms = all_terms(rest, near, w_in, False)
     w_out = load(after(w_out, w_in))
-    grad_terms, _, _ = gather_tokens(after(grad_line, up, down), w_out, True)
-    pre = reduce_rows(terms)
-    grad_act = reduce_rows(grad_terms)
-    act = gelu_value(pre).astype(jnp.bfloat16)
-    grad_pre = (grad_act * gelu_slope(pre)).astype(jnp.bfloat16)
-    outputs = reduce_tokens(gather_rows(act, w_out, False))
-    in_grad = reduce_tokens(gather_rows(grad_pre, w_in, True))
+    both = rounded(terms[512:], swap(terms[:512]))
+    far = send(both[256:384], along_y)
+    grad_rest = ring_rest(grad_up, grad_down)
+    grad_near = near_terms(grad_line, after(grad_up, terms), grad_down, w_out, True)
+    grad_terms = all_terms(grad_rest, grad_near, w_out, True)
+    arrived = send(add_far(both, far), along_y)
+    grad_both = rounded(grad_terms[512:], swap(grad_terms[:512]))
+    mine = add_own(arrived, both)
+    grad_far = send(grad_both[256:384], along_y)
+    grad_arrived = send(add_far(grad_both, grad_far), along_y)
+    pre = add_other(mine, swap(mine))
+    act, slope = lax.optimization_barrier((gelu_value(pre).astype(jnp.bfloat16), gelu_slope(pre)))
+    grad_mine = add_own(grad_arrived, grad_both)
+    act_near = send(act, along_y)
+    grad_act = add_other(grad_mine, swap(grad_mine))
+    grad_pre = (grad_act * slope).astype(jnp.bfloat16)
+    grad_pre_near = send(grad_pre, along_y)
+    act_far = send(act_near[:128], along_y)
+    act_other_near = swap(act_near)
+    early = early_sums(act, act_near, w_out, False)
+    grad_pre_far = send(grad_pre_near[:128], along_y)
+    grad_pre_other_near = swap(grad_pre_near)
+    grad_early = early_sums(grad_pre, grad_pre_near, w_in, True)
+    act_other_far = send(act_far, other_core)
+    sums = all_sums(act_other_near, act_far, act_other_far, early, w_out, False)
+    parts = cut(sums, 4)
+    grad_pre_far = after(grad_pre_far, sums)
+    grad_pre_other_far = send(grad_pre_far, other_core)
+    outer = pass_far(parts)
+    inner = pass_near(parts, *outer)
+    grad_sums = all_sums(
+        grad_pre_other_near, grad_pre_far, grad_pre_other_far, grad_early, w_in, True
+    )
+    out_line = rounded(parts[0], *inner)
+    grad_parts = cut(grad_sums, 4)
+    grad_outer = pass_far(grad_parts)
+    outputs = finish(out_line)
+    grad_inner = pass_near(grad_parts, *grad_outer)
+    in_grad = finish(rounded(grad_parts[0], *grad_inner))
     return (outputs, in_grad)
 
 

time: 179 us -> 172 us (0.961)
  starting transfers between devices: 51.4 us -> 45.2 us
    ppermute x44 -> x43, starting transfers between devices: 51.4 us -> 45.2 us  [send(): return lax.ppermute(value, AXES, device_pairs(move))]
    unnamed x11, local copies, waits for them, and re-layouts: 3.36 us -> 1.03 us
    ppermute x44 -> x43, waiting for transfers between devices: 94.4 us -> 94.8 us  [send(): return lax.ppermute(value, AXES, device_pairs(move))]
  transfers between devices with their start and end apart: 44 -> 43, of which waited for: 22 -> 21; matrix products, arithmetic and copies ran while one was open for 3% -> 3% of each run, Pallas kernels for 12% -> 13%
where the time goes in v3:
time: 172 us
  waiting for transfers between devices  94.8 us (55%)
  starting transfers between devices  45.2 us (26%)
  Pallas kernels  22.4 us (13%)
  other arithmetic  5.62 us (3%)
  local copies, waits for them, and re-layouts  2.97 us (2%)
    ppermute x43, waiting for transfers between devices, send(): return lax.ppermute(value, AXES, device_pairs(move))  94.8 us
    ppermute x43, starting transfers between devices, send(): return lax.ppermute(value, AXES, device_pairs(move))  45.2 us
    pallas_call x8, Pallas kernels, matmul(): pl.pallas_call(functools.partial(matmul_kernel, transposed, places, forme...  21.7 us
    convert_element_type x12, other arithmetic, rounded(): return sum_parts(*parts).astype(jnp.bfloat16)  3.66 us
  transfers between devices with their start and end apart: 43, of which 21 were waited for; matrix products, arithmetic and copies ran while one was open for 3% of the time, Pallas kernels for 13%

profile of v3, /device:TPU:0, one launch (start us, length us, event | category | flops | bytes accessed | tf_op | source)
XLA Modules:
  0.0 172.1 jit_solution(15809071730430433478)
XLA Ops:
  2.6 2.9 %collective-permute-start = (bf16[128,1536]{1,0:T(8,128)(2,1)S(1)}, bf16[128,1536]{1,0:T(8,128)(2,1)S(1)}, u32[]{:S(2)}, u32[]{:S(2)}) collective-permute-start(bf16[128,1536]{1,0:T(8,128)(2,1)S(1)} %constant_dynamic-update-slice_fusion), channel_id=1, source_target_pairs={{0,3},{1,0},{2,1},{3,2},{4,100},{5,101},{6,102},{7,103},{8,11},{9,... | collective-permute-start | bytes 1179656 | tf_op jit(solution)/shard_map/ppermute | solution.py:42
  7.2 7.8 %collective-permute-done = bf16[128,1536]{1,0:T(8,128)(2,1)S(1)} collective-permute-done((bf16[128,1536]{1,0:T(8,128)(2,1)S(1)}, bf16[128,1536]{1,0:T(8,128)(2,1)S(1)}, u32[]{:S(2)}, u32[]{:S(2)}) %collective-permute-start) | collective-permute-done | bytes 393248 | tf_op jit(solution)/shard_map/ppermute | solution.py:42
  15.1 3.9 %collective-permute-done.2 = bf16[128,1536]{1,0:T(8,128)(2,1)S(1)} collective-permute-done((bf16[128,1536]{1,0:T(8,128)(2,1)S(1)}, bf16[128,1536]{1,0:T(8,128)(2,1)S(1)}, u32[]{:S(2)}, u32[]{:S(2)}) %collective-permute-start.2) | collective-permute-done | bytes 393248 | tf_op jit(solution)/shard_map/ppermute | solution.py:42
  25.8 7.4 %collective-permute-done.5.refs_2_ = bf16[256,1536]{1,0:T(8,128)(2,1)S(1)} collective-permute-done((bf16[256,1536]{1,0:T(8,128)(2,1)S(1)}, bf16[256,1536]{1,0:T(8,128)(2,1)S(1)}, u32[]{:S(2)}, u32[]{:S(2)}) %collective-permute-start.5) | collective-permute-done | bytes 786464 | tf_op jit(solution)/shard_map/ppermute | solution.py:42
  33.3 3.3 %collective-permute-start.4 = (bf16[128,1536]{1,0:T(8,128)(2,1)S(1)}, bf16[128,1536]{1,0:T(8,128)(2,1)S(1)}, u32[]{:S(2)}, u32[]{:S(2)}) collective-permute-start(bf16[128,1536]{1,0:T(8,128)(2,1)S(1)} %slice.195), channel_id=1, source_target_pairs={{0,96},{1,97},{2,98},{3,99},{4,7},{5,4},{6,5},{7,6},{8,104},{9,105... | collective-permute-start | bytes 1179656 | tf_op jit(solution)/shard_map/ppermute | solution.py:42
  36.6 3.8 %shard_map.60.refs_3_ = bf16[768,1536]{1,0:T(8,128)(2,1)S(1)} custom-call(bf16[256,1536]{1,0:T(8,128)(2,1)S(1)} %pad_maximum_fusion.refs_0_, bf16[256,1536]{1,0:T(8,128)(2,1)S(1)} %collective-permute-done.3.refs_1_, bf16[256,1536]{1,0:T(8,128)(2,1)S(1)} %collective-permute-done.5.refs_2_, bf16[1536,1536]{1,0:T(8,128)(2,1)S(1)} %shard_map.59.refs_3_.refs_2_), custom_call_target="tpu_custom_call" | custom-call | flops 1 | bytes 1 | tf_op jit(solution)/shard_map/pallas_call | solution.py:163
  41.6 3.4 %collective-permute-start.24 = (bf16[128,1536]{1,0:T(8,128)(2,1)S(1)}, bf16[128,1536]{1,0:T(8,128)(2,1)S(1)}, u32[]{:S(2)}, u32[]{:S(2)}) collective-permute-start(bf16[128,1536]{1,0:T(8,128)(2,1)S(1)} %slice.223), channel_id=1, source_target_pairs={{0,96},{1,97},{2,98},{3,99},{4,7},{5,4},{6,5},{7,6},{8,104},{9,105... | collective-permute-start | bytes 1179656 | tf_op jit(solution)/shard_map/ppermute | solution.py:42
  48.5 3.8 %shard_map.65.refs_3_ = bf16[768,1536]{1,0:T(8,128)(2,1)S(1)} custom-call(bf16[256,1536]{1,0:T(8,128)(2,1)S(1)} %pad_maximum_fusion.6.refs_0_, bf16[256,1536]{1,0:T(8,128)(2,1)S(1)} %collective-permute-done.23.refs_1_, bf16[256,1536]{1,0:T(8,128)(2,1)S(1)} %collective-permute-done.25.refs_2_, bf16[1536,1536]{1,0:T(8,128)(2,1)S(1)} %shard_map.62.refs_2_.refs_3_), custom_call_target="tpu_custom_call" | custom-call | flops 1 | bytes 1 | tf_op jit(solution)/shard_map/pallas_call | solution.py:163
  61.5 4.5 %collective-permute-done.9 = bf16[128,1536]{1,0:T(8,128)(2,1)S(1)} collective-permute-done((bf16[128,1536]{1,0:T(8,128)(2,1)S(1)}, bf16[128,1536]{1,0:T(8,128)(2,1)S(1)}, u32[]{:S(2)}, u32[]{:S(2)}) %collective-permute-start.9) | collective-permute-done | bytes 393248 | tf_op jit(solution)/shard_map/ppermute | solution.py:42
  66.6 3.6 %collective-permute-done.29 = bf16[128,1536]{1,0:T(8,128)(2,1)S(1)} collective-permute-done((bf16[128,1536]{1,0:T(8,128)(2,1)S(1)}, bf16[128,1536]{1,0:T(8,128)(2,1)S(1)}, u32[]{:S(2)}, u32[]{:S(2)}) %collective-permute-start.29) | collective-permute-done | bytes 393248 | tf_op jit(solution)/shard_map/ppermute | solution.py:42
  70.8 8.6 %collective-permute-done.10 = bf16[256,1536]{1,0:T(8,128)(2,1)S(1)} collective-permute-done((bf16[256,1536]{1,0:T(8,128)(2,1)S(1)}, bf16[256,1536]{1,0:T(8,128)(2,1)S(1)}, u32[]{:S(2)}, u32[]{:S(2)}) %collective-permute-start.10) | collective-permute-done | bytes 786464 | tf_op jit(solution)/shard_map/ppermute | solution.py:42
  79.7 8.1 %collective-permute-done.30 = bf16[256,1536]{1,0:T(8,128)(2,1)S(1)} collective-permute-done((bf16[256,1536]{1,0:T(8,128)(2,1)S(1)}, bf16[256,1536]{1,0:T(8,128)(2,1)S(1)}, u32[]{:S(2)}, u32[]{:S(2)}) %collective-permute-start.30) | collective-permute-done | bytes 786464 | tf_op jit(solution)/shard_map/ppermute | solution.py:42
  91.0 11.6 %collective-permute-done.12.refs_1_ = bf16[256,1536]{1,0:T(8,128)(2,1)S(1)} collective-permute-done((bf16[256,1536]{1,0:T(8,128)(2,1)S(1)}, bf16[256,1536]{1,0:T(8,128)(2,1)S(1)}, u32[]{:S(2)}, u32[]{:S(2)}) %collective-permute-start.12) | collective-permute-done | bytes 786464 | tf_op jit(solution)/shard_map/ppermute | solution.py:42
  102.8 12.4 %collective-permute-done.14.refs_1_ = bf16[128,1536]{1,0:T(8,128)(2,1)S(1)} collective-permute-done((bf16[128,1536]{1,0:T(8,128)(2,1)S(1)}, bf16[128,1536]{1,0:T(8,128)(2,1)S(1)}, u32[]{:S(2)}, u32[]{:S(2)}) %collective-permute-start.14) | collective-permute-done | bytes 393248 | tf_op jit(solution)/shard_map/ppermute | solution.py:42
  116.2 2.6 %shard_map.67.refs_4_ = bf16[512,1536]{1,0:T(8,128)(2,1)S(1)} custom-call(bf16[256,1536]{1,0:T(8,128)(2,1)S(1)} %multiply_convert_fusion.refs_0_, bf16[256,1536]{1,0:T(8,128)(2,1)S(1)} %collective-permute-done.32.refs_1_, bf16[1536,1536]{1,0:T(8,128)(2,1)S(1)} %shard_map.59.refs_3_.refs_2_), custom_call_target="tpu_custom_call" | custom-call | flops 1 | bytes 1 | tf_op jit(solution)/shard_map/pallas_call | solution.py:163
  121.4 2.8 %shard_map.64 = bf16[1024,1536]{1,0:T(8,128)(2,1)S(1)} custom-call(bf16[256,1536]{1,0:T(8,128)(2,1)S(1)} %collective-permute-done.13.refs_0_, bf16[128,1536]{1,0:T(8,128)(2,1)S(1)} %collective-permute-done.14.refs_1_, bf16[128,1536]{1,0:T(8,128)(2,1)S(1)} %collective-permute-done.15.refs_2_, bf16[1536,1536]{1,0:T(8,128)(2,1)S(1)} %shard_map.62.refs_2_.refs_3_, ...), custom_call_target="tpu_custom_call" | custom-call | flops 1 | bytes 1 | tf_op jit(solution)/shard_map/pallas_call | solution.py:163
  124.8 3.2 %collective-permute-start.18 = (bf16[128,1536]{1,0:T(8,128)(2,1)S(1)}, bf16[128,1536]{1,0:T(8,128)(2,1)S(1)}, u32[]{:S(2)}, u32[]{:S(2)}) collective-permute-start(bf16[128,1536]{1,0:T(8,128)(2,1)S(1)} %get-tuple-element.33), channel_id=1, source_target_pairs={{0,96},{1,97},{2,98},{3,99},{4,7},{5,4},{6,5},{7,6},{8,104},{9,105... | collective-permute-start | bytes 1179656 | tf_op jit(solution)/shard_map/ppermute | solution.py:42
  128.0 2.8 %shard_map.68 = bf16[1024,1536]{1,0:T(8,128)(2,1)S(1)} custom-call(bf16[256,1536]{1,0:T(8,128)(2,1)S(1)} %collective-permute-done.33.refs_0_, bf16[128,1536]{1,0:T(8,128)(2,1)S(1)} %collective-permute-done.34.refs_1_, bf16[128,1536]{1,0:T(8,128)(2,1)S(1)} %collective-permute-done.35.refs_2_, bf16[1536,1536]{1,0:T(8,128)(2,1)S(1)} %shard_map.59.refs_3_.refs_2_, ...), custom_call_target="tpu_custom_call" | custom-call | flops 1 | bytes 1 | tf_op jit(solution)/shard_map/pallas_call | solution.py:163
  131.0 3.2 %collective-permute-start.38 = (bf16[128,1536]{1,0:T(8,128)(2,1)S(1)}, bf16[128,1536]{1,0:T(8,128)(2,1)S(1)}, u32[]{:S(2)}, u32[]{:S(2)}) collective-permute-start(bf16[128,1536]{1,0:T(8,128)(2,1)S(1)} %get-tuple-element.25), channel_id=1, source_target_pairs={{0,96},{1,97},{2,98},{3,99},{4,7},{5,4},{6,5},{7,6},{8,104},{9,105... | collective-permute-start | bytes 1179656 | tf_op jit(solution)/shard_map/ppermute | solution.py:42
  134.6 3.3 %collective-permute-start.19 = (bf16[256,1536]{1,0:T(8,128)(2,1)S(1)}, bf16[256,1536]{1,0:T(8,128)(2,1)S(1)}, u32[]{:S(2)}, u32[]{:S(2)}) collective-permute-start(bf16[256,1536]{1,0:T(8,128)(2,1)S(1)} %pad_maximum_fusion.5), channel_id=1, source_target_pairs={{0,96},{1,97},{2,98},{3,99},{4,7},{5,4},{6,5},{7,6},{8,104},{9,105... | collective-permute-start | bytes 2359304 | tf_op jit(solution)/shard_map/ppermute | solution.py:42
  140.4 3.3 %collective-permute-start.39 = (bf16[256,1536]{1,0:T(8,128)(2,1)S(1)}, bf16[256,1536]{1,0:T(8,128)(2,1)S(1)}, u32[]{:S(2)}, u32[]{:S(2)}) collective-permute-start(bf16[256,1536]{1,0:T(8,128)(2,1)S(1)} %pad_maximum_fusion.10), channel_id=1, source_target_pairs={{0,96},{1,97},{2,98},{3,99},{4,7},{5,4},{6,5},{7,6},{8,104},{9,105... | collective-permute-start | bytes 2359304 | tf_op jit(solution)/shard_map/ppermute | solution.py:42
  143.7 4.7 %collective-permute-done.17 = bf16[256,1536]{1,0:T(8,128)(2,1)S(1)} collective-permute-done((bf16[256,1536]{1,0:T(8,128)(2,1)S(1)}, bf16[256,1536]{1,0:T(8,128)(2,1)S(1)}, u32[]{:S(2)}, u32[]{:S(2)}) %collective-permute-start.17) | collective-permute-done | bytes 786464 | tf_op jit(solution)/shard_map/ppermute | solution.py:42
  152.5 8.5 %collective-permute-done.37 = bf16[256,1536]{1,0:T(8,128)(2,1)S(1)} collective-permute-done((bf16[256,1536]{1,0:T(8,128)(2,1)S(1)}, bf16[256,1536]{1,0:T(8,128)(2,1)S(1)}, u32[]{:S(2)}, u32[]{:S(2)}) %collective-permute-start.37) | collective-permute-done | bytes 786464 | tf_op jit(solution)/shard_map/ppermute | solution.py:42
  165.7 4.8 %collective-permute-done.40 = bf16[64,1536]{1,0:T(8,128)(2,1)S(1)} collective-permute-done((bf16[64,1536]{1,0:T(8,128)(2,1)S(1)}, bf16[64,1536]{1,0:T(8,128)(2,1)S(1)}, u32[]{:S(2)}, u32[]{:S(2)}) %collective-permute-start.40) | collective-permute-done | bytes 196640 | tf_op jit(solution)/shard_map/ppermute | solution.py:42
  (130 shorter events, 46.4 us)
Async XLA Ops:
  2.6 12.4 %collective-permute-start = (bf16[128,1536]{1,0:T(8,128)(2,1)S(1)}, bf16[128,1536]{1,0:T(8,128)(2,1)S(1)}, u32[]{:S(2)}, u32[]{:S(2)}) collective-permute-start(bf16[128,1536]{1,0:T(8,128)(2,1)S(1)} %constant_dynamic-update-slice_fusion), channel_id=1, source_target_pairs={{0,3},{1,0},{2,1},{3,2},{4,100},{5,101},{6,102},{7,103},{8,11},{9,... | collective-permute-start | bytes 1179656 | tf_op jit(solution)/shard_map/ppermute | solution.py:42
  6.3 12.7 %collective-permute-start.2 = (bf16[128,1536]{1,0:T(8,128)(2,1)S(1)}, bf16[128,1536]{1,0:T(8,128)(2,1)S(1)}, u32[]{:S(2)}, u32[]{:S(2)}) collective-permute-start(bf16[128,1536]{1,0:T(8,128)(2,1)S(1)} %constant_dynamic-update-slice_fusion), channel_id=1, source_target_pairs={{0,1},{1,2},{2,3},{3,0},{4,36},{5,37},{6,38},{7,39},{8,9},{9,10},{... | collective-permute-start | bytes 1179656 | tf_op jit(solution)/shard_map/ppermute | solution.py:42
  19.1 14.1 %collective-permute-start.5 = (bf16[256,1536]{1,0:T(8,128)(2,1)S(1)}, bf16[256,1536]{1,0:T(8,128)(2,1)S(1)}, u32[]{:S(2)}, u32[]{:S(2)}) collective-permute-start(bf16[256,1536]{1,0:T(8,128)(2,1)S(1)} %pad_maximum_fusion.refs_0_), channel_id=1, source_target_pairs={{0,32},{1,33},{2,34},{3,35},{4,5},{5,6},{6,7},{7,4},{8,40},{9,41},... | collective-permute-start | bytes 2359304 | tf_op jit(solution)/shard_map/ppermute | solution.py:42
  21.1 12.2 %collective-permute-start.3 = (bf16[256,1536]{1,0:T(8,128)(2,1)S(1)}, bf16[256,1536]{1,0:T(8,128)(2,1)S(1)}, u32[]{:S(2)}, u32[]{:S(2)}) collective-permute-start(bf16[256,1536]{1,0:T(8,128)(2,1)S(1)} %pad_maximum_fusion.refs_0_), channel_id=1, source_target_pairs={{0,96},{1,97},{2,98},{3,99},{4,7},{5,4},{6,5},{7,6},{8,104},{9,105... | collective-permute-start | bytes 2359304 | tf_op jit(solution)/shard_map/ppermute | solution.py:42
  23.3 18.2 %collective-permute-start.23 = (bf16[256,1536]{1,0:T(8,128)(2,1)S(1)}, bf16[256,1536]{1,0:T(8,128)(2,1)S(1)}, u32[]{:S(2)}, u32[]{:S(2)}) collective-permute-start(bf16[256,1536]{1,0:T(8,128)(2,1)S(1)} %pad_maximum_fusion.6.refs_0_), channel_id=1, source_target_pairs={{0,96},{1,97},{2,98},{3,99},{4,7},{5,4},{6,5},{7,6},{8,104},{9,105... | collective-permute-start | bytes 2359304 | tf_op jit(solution)/shard_map/ppermute | solution.py:42
  25.4 16.2 %collective-permute-start.25 = (bf16[256,1536]{1,0:T(8,128)(2,1)S(1)}, bf16[256,1536]{1,0:T(8,128)(2,1)S(1)}, u32[]{:S(2)}, u32[]{:S(2)}) collective-permute-start(bf16[256,1536]{1,0:T(8,128)(2,1)S(1)} %pad_maximum_fusion.6.refs_0_), channel_id=1, source_target_pairs={{0,32},{1,33},{2,34},{3,35},{4,5},{5,6},{6,7},{7,4},{8,40},{9,41},... | collective-permute-start | bytes 2359304 | tf_op jit(solution)/shard_map/ppermute | solution.py:42
  33.2 12.6 %collective-permute-start.6 = (bf16[128,1536]{1,0:T(8,128)(2,1)S(1)}, bf16[128,1536]{1,0:T(8,128)(2,1)S(1)}, u32[]{:S(2)}, u32[]{:S(2)}) collective-permute-start(bf16[128,1536]{1,0:T(8,128)(2,1)S(1)} %slice.196), channel_id=1, source_target_pairs={{0,32},{1,33},{2,34},{3,35},{4,5},{5,6},{6,7},{7,4},{8,40},{9,41},... | collective-permute-start | bytes 1179656 | tf_op jit(solution)/shard_map/ppermute | solution.py:42
  33.3 12.5 %collective-permute-start.4 = (bf16[128,1536]{1,0:T(8,128)(2,1)S(1)}, bf16[128,1536]{1,0:T(8,128)(2,1)S(1)}, u32[]{:S(2)}, u32[]{:S(2)}) collective-permute-start(bf16[128,1536]{1,0:T(8,128)(2,1)S(1)} %slice.195), channel_id=1, source_target_pairs={{0,96},{1,97},{2,98},{3,99},{4,7},{5,4},{6,5},{7,6},{8,104},{9,105... | collective-permute-start | bytes 1179656 | tf_op jit(solution)/shard_map/ppermute | solution.py:42
  41.6 10.7 %collective-permute-start.24 = (bf16[128,1536]{1,0:T(8,128)(2,1)S(1)}, bf16[128,1536]{1,0:T(8,128)(2,1)S(1)}, u32[]{:S(2)}, u32[]{:S(2)}) collective-permute-start(bf16[128,1536]{1,0:T(8,128)(2,1)S(1)} %slice.223), channel_id=1, source_target_pairs={{0,96},{1,97},{2,98},{3,99},{4,7},{5,4},{6,5},{7,6},{8,104},{9,105... | collective-permute-start | bytes 1179656 | tf_op jit(solution)/shard_map/ppermute | solution.py:42
  59.8 10.4 %collective-permute-start.29 = (bf16[128,1536]{1,0:T(8,128)(2,1)S(1)}, bf16[128,1536]{1,0:T(8,128)(2,1)S(1)}, u32[]{:S(2)}, u32[]{:S(2)}) collective-permute-start(bf16[128,1536]{1,0:T(8,128)(2,1)S(1)} %get-tuple-element.38), channel_id=1, source_target_pairs={{0,8},{1,9},{2,10},{3,11},{4,28},{5,29},{6,30},{7,31},{8,16},{9,17... | collective-permute-start | bytes 1179656 | tf_op jit(solution)/shard_map/ppermute | solution.py:42
  66.1 13.3 %collective-permute-start.10 = (bf16[256,1536]{1,0:T(8,128)(2,1)S(1)}, bf16[256,1536]{1,0:T(8,128)(2,1)S(1)}, u32[]{:S(2)}, u32[]{:S(2)}) collective-permute-start(bf16[256,1536]{1,0:T(8,128)(2,1)S(1)} %pad_maximum_fusion.1), channel_id=1, source_target_pairs={{0,8},{1,9},{2,10},{3,11},{4,28},{5,29},{6,30},{7,31},{8,16},{9,17... | collective-permute-start | bytes 2359304 | tf_op jit(solution)/shard_map/ppermute | solution.py:42
  70.4 17.5 %collective-permute-start.30 = (bf16[256,1536]{1,0:T(8,128)(2,1)S(1)}, bf16[256,1536]{1,0:T(8,128)(2,1)S(1)}, u32[]{:S(2)}, u32[]{:S(2)}) collective-permute-start(bf16[256,1536]{1,0:T(8,128)(2,1)S(1)} %pad_maximum_fusion.7), channel_id=1, source_target_pairs={{0,8},{1,9},{2,10},{3,11},{4,28},{5,29},{6,30},{7,31},{8,16},{9,17... | collective-permute-start | bytes 2359304 | tf_op jit(solution)/shard_map/ppermute | solution.py:42
  89.3 13.3 %collective-permute-start.12 = (bf16[256,1536]{1,0:T(8,128)(2,1)S(1)}, bf16[256,1536]{1,0:T(8,128)(2,1)S(1)}, u32[]{:S(2)}, u32[]{:S(2)}) collective-permute-start(bf16[256,1536]{1,0:T(8,128)(2,1)S(1)} %get-tuple-element.15.refs_0_), channel_id=1, source_target_pairs={{0,8},{1,9},{2,10},{3,11},{4,28},{5,29},{6,30},{7,31},{8,16},{9,17... | collective-permute-start | bytes 2359304 | tf_op jit(solution)/shard_map/ppermute | solution.py:42
  90.7 24.5 %collective-permute-start.32 = (bf16[256,1536]{1,0:T(8,128)(2,1)S(1)}, bf16[256,1536]{1,0:T(8,128)(2,1)S(1)}, u32[]{:S(2)}, u32[]{:S(2)}) collective-permute-start(bf16[256,1536]{1,0:T(8,128)(2,1)S(1)} %multiply_convert_fusion.refs_0_), channel_id=1, source_target_pairs={{0,8},{1,9},{2,10},{3,11},{4,28},{5,29},{6,30},{7,31},{8,16},{9,17... | collective-permute-start | bytes 2359304 | tf_op jit(solution)/shard_map/ppermute | solution.py:42
  102.6 12.6 %collective-permute-start.14 = (bf16[128,1536]{1,0:T(8,128)(2,1)S(1)}, bf16[128,1536]{1,0:T(8,128)(2,1)S(1)}, u32[]{:S(2)}, u32[]{:S(2)}) collective-permute-start(bf16[128,1536]{1,0:T(8,128)(2,1)S(1)} %slice.262), channel_id=1, source_target_pairs={{0,8},{1,9},{2,10},{3,11},{4,28},{5,29},{6,30},{7,31},{8,16},{9,17... | collective-permute-start | bytes 1179656 | tf_op jit(solution)/shard_map/ppermute | solution.py:42
  102.7 18.7 %collective-permute-start.13 = (bf16[256,1536]{1,0:T(8,128)(2,1)S(1)}, bf16[256,1536]{1,0:T(8,128)(2,1)S(1)}, u32[]{:S(2)}, u32[]{:S(2)}) collective-permute-start(bf16[256,1536]{1,0:T(8,128)(2,1)S(1)} %collective-permute-done.12.refs_1_), channel_id=1, source_target_pairs={{0,4},{1,5},{2,6},{3,7},{4,0},{5,1},{6,2},{7,3},{8,12},{9,13},{10,... | collective-permute-start | bytes 2359304 | tf_op jit(solution)/shard_map/ppermute | solution.py:42
  115.6 12.4 %collective-permute-start.33 = (bf16[256,1536]{1,0:T(8,128)(2,1)S(1)}, bf16[256,1536]{1,0:T(8,128)(2,1)S(1)}, u32[]{:S(2)}, u32[]{:S(2)}) collective-permute-start(bf16[256,1536]{1,0:T(8,128)(2,1)S(1)} %collective-permute-done.32.refs_1_), channel_id=1, source_target_pairs={{0,4},{1,5},{2,6},{3,7},{4,0},{5,1},{6,2},{7,3},{8,12},{9,13},{10,... | collective-permute-start | bytes 2359304 | tf_op jit(solution)/shard_map/ppermute | solution.py:42
  134.5 13.9 %collective-permute-start.17 = (bf16[256,1536]{1,0:T(8,128)(2,1)S(1)}, bf16[256,1536]{1,0:T(8,128)(2,1)S(1)}, u32[]{:S(2)}, u32[]{:S(2)}) collective-permute-start(bf16[256,1536]{1,0:T(8,128)(2,1)S(1)} %pad_maximum_fusion.4), channel_id=1, source_target_pairs={{0,32},{1,33},{2,34},{3,35},{4,5},{5,6},{6,7},{7,4},{8,40},{9,41},... | collective-permute-start | bytes 2359304 | tf_op jit(solution)/shard_map/ppermute | solution.py:42
  134.6 13.8 %collective-permute-start.19 = (bf16[256,1536]{1,0:T(8,128)(2,1)S(1)}, bf16[256,1536]{1,0:T(8,128)(2,1)S(1)}, u32[]{:S(2)}, u32[]{:S(2)}) collective-permute-start(bf16[256,1536]{1,0:T(8,128)(2,1)S(1)} %pad_maximum_fusion.5), channel_id=1, source_target_pairs={{0,96},{1,97},{2,98},{3,99},{4,7},{5,4},{6,5},{7,6},{8,104},{9,105... | collective-permute-start | bytes 2359304 | tf_op jit(solution)/shard_map/ppermute | solution.py:42
  140.2 20.8 %collective-permute-start.37 = (bf16[256,1536]{1,0:T(8,128)(2,1)S(1)}, bf16[256,1536]{1,0:T(8,128)(2,1)S(1)}, u32[]{:S(2)}, u32[]{:S(2)}) collective-permute-start(bf16[256,1536]{1,0:T(8,128)(2,1)S(1)} %pad_maximum_fusion.9), channel_id=1, source_target_pairs={{0,32},{1,33},{2,34},{3,35},{4,5},{5,6},{6,7},{7,4},{8,40},{9,41},... | collective-permute-start | bytes 2359304 | tf_op jit(solution)/shard_map/ppermute | solution.py:42
  140.4 20.7 %collective-permute-start.39 = (bf16[256,1536]{1,0:T(8,128)(2,1)S(1)}, bf16[256,1536]{1,0:T(8,128)(2,1)S(1)}, u32[]{:S(2)}, u32[]{:S(2)}) collective-permute-start(bf16[256,1536]{1,0:T(8,128)(2,1)S(1)} %pad_maximum_fusion.10), channel_id=1, source_target_pairs={{0,96},{1,97},{2,98},{3,99},{4,7},{5,4},{6,5},{7,6},{8,104},{9,105... | collective-permute-start | bytes 2359304 | tf_op jit(solution)/shard_map/ppermute | solution.py:42
  148.8 14.3 %collective-permute-start.20 = (bf16[64,1536]{1,0:T(8,128)(2,1)S(1)}, bf16[64,1536]{1,0:T(8,128)(2,1)S(1)}, u32[]{:S(2)}, u32[]{:S(2)}) collective-permute-start(bf16[64,1536]{1,0:T(8,128)(2,1)S(1)} %get-tuple-element.49), channel_id=1, source_target_pairs={{0,1},{1,2},{2,3},{3,0},{4,36},{5,37},{6,38},{7,39},{8,9},{9,10},{... | collective-permute-start | bytes 589832 | tf_op jit(solution)/shard_map/ppermute | solution.py:42
  149.1 15.8 %collective-permute-start.21 = (bf16[64,1536]{1,0:T(8,128)(2,1)S(1)}, bf16[64,1536]{1,0:T(8,128)(2,1)S(1)}, u32[]{:S(2)}, u32[]{:S(2)}) collective-permute-start(bf16[64,1536]{1,0:T(8,128)(2,1)S(1)} %get-tuple-element.51), channel_id=1, source_target_pairs={{0,2},{1,3},{2,0},{3,1},{4,68},{5,69},{6,70},{7,71},{8,10},{9,11},... | collective-permute-start | bytes 589832 | tf_op jit(solution)/shard_map/ppermute | solution.py:42
  151.2 13.8 %collective-permute-start.22 = (bf16[64,1536]{1,0:T(8,128)(2,1)S(1)}, bf16[64,1536]{1,0:T(8,128)(2,1)S(1)}, u32[]{:S(2)}, u32[]{:S(2)}) collective-permute-start(bf16[64,1536]{1,0:T(8,128)(2,1)S(1)} %get-tuple-element.50), channel_id=1, source_target_pairs={{0,3},{1,0},{2,1},{3,2},{4,100},{5,101},{6,102},{7,103},{8,11},{9,... | collective-permute-start | bytes 589832 | tf_op jit(solution)/shard_map/ppermute | solution.py:42
  (24 other events, 187.9 us)

commit v4 on v3

--- a/solution.py
+++ b/solution.py
@@ -201,7 +201,12 @@
 
 
 def gather_lines(own, grad_own):
-    both = jnp.concatenate([own, grad_own])
+    wide = [(0, BLOCK, 0), (0, 0, 0)]
+    upper = lax.broadcasted_iota(jnp.int32, (2 * BLOCK, own.shape[1]), 0) < BLOCK
+    zero = jnp.zeros((), own.dtype)
+    both = jnp.where(
+        upper, lax.pad(own, zero, wide), lax.pad(grad_own, zero, [(BLOCK, 0, 0), (0, 0, 0)])
+    )
     parts = [send(both, first_axis(-k)) for k in (1, 2, 3)]
     line = jnp.concatenate([own] + [part[:BLOCK] for part in parts])
     return line, jnp.concatenate([grad_own] + [part[BLOCK:] for part in parts])

time: 172 us -> 172 us (level)
  local copies, waits for them, and re-layouts: 2.97 us -> 1.03 us
where the time goes in v4:
time: 172 us; the launch traced here: 171 us
  waiting for transfers between devices  94.8 us (55%)
  starting transfers between devices  45.1 us (26%)
  Pallas kernels  22.4 us (13%)
  other arithmetic  6.82 us (4%)
    ppermute x43, waiting for transfers between devices, send(): return lax.ppermute(value, AXES, device_pairs(move))  94.8 us
    ppermute x43, starting transfers between devices, send(): return lax.ppermute(value, AXES, device_pairs(move))  45.1 us
    pallas_call x8, Pallas kernels, matmul(): pl.pallas_call(functools.partial(matmul_kernel, transposed, places, forme...  21.7 us
    convert_element_type x12, other arithmetic, rounded(): return sum_parts(*parts).astype(jnp.bfloat16)  3.66 us
  transfers between devices with their start and end apart: 43, of which 21 were waited for; matrix products, arithmetic and copies ran while one was open for 3% of the time, Pallas kernels for 13%

profile of v4, /device:TPU:0, one launch (start us, length us, event | category | flops | bytes accessed | tf_op | source)
XLA Modules:
  0.0 171.4 jit_solution(1670806965076579564)
XLA Ops:
  1.9 2.9 %collective-permute-start = (bf16[128,1536]{1,0:T(8,128)(2,1)S(1)}, bf16[128,1536]{1,0:T(8,128)(2,1)S(1)}, u32[]{:S(2)}, u32[]{:S(2)}) collective-permute-start(bf16[128,1536]{1,0:T(8,128)(2,1)S(1)} %pad_select_fusion), channel_id=1, source_target_pairs={{0,3},{1,0},{2,1},{3,2},{4,100},{5,101},{6,102},{7,103},{8,11},{9,... | collective-permute-start | bytes 1179656 | tf_op jit(solution)/shard_map/ppermute | solution.py:42
  6.5 7.8 %collective-permute-done = bf16[128,1536]{1,0:T(8,128)(2,1)S(1)} collective-permute-done((bf16[128,1536]{1,0:T(8,128)(2,1)S(1)}, bf16[128,1536]{1,0:T(8,128)(2,1)S(1)}, u32[]{:S(2)}, u32[]{:S(2)}) %collective-permute-start) | collective-permute-done | bytes 393248 | tf_op jit(solution)/shard_map/ppermute | solution.py:42
  14.4 3.9 %collective-permute-done.2 = bf16[128,1536]{1,0:T(8,128)(2,1)S(1)} collective-permute-done((bf16[128,1536]{1,0:T(8,128)(2,1)S(1)}, bf16[128,1536]{1,0:T(8,128)(2,1)S(1)}, u32[]{:S(2)}, u32[]{:S(2)}) %collective-permute-start.2) | collective-permute-done | bytes 393248 | tf_op jit(solution)/shard_map/ppermute | solution.py:42
  25.0 7.4 %collective-permute-done.5.refs_2_ = bf16[256,1536]{1,0:T(8,128)(2,1)S(1)} collective-permute-done((bf16[256,1536]{1,0:T(8,128)(2,1)S(1)}, bf16[256,1536]{1,0:T(8,128)(2,1)S(1)}, u32[]{:S(2)}, u32[]{:S(2)}) %collective-permute-start.5) | collective-permute-done | bytes 786464 | tf_op jit(solution)/shard_map/ppermute | solution.py:42
  32.6 3.3 %collective-permute-start.4 = (bf16[128,1536]{1,0:T(8,128)(2,1)S(1)}, bf16[128,1536]{1,0:T(8,128)(2,1)S(1)}, u32[]{:S(2)}, u32[]{:S(2)}) collective-permute-start(bf16[128,1536]{1,0:T(8,128)(2,1)S(1)} %slice.195), channel_id=1, source_target_pairs={{0,96},{1,97},{2,98},{3,99},{4,7},{5,4},{6,5},{7,6},{8,104},{9,105... | collective-permute-start | bytes 1179656 | tf_op jit(solution)/shard_map/ppermute | solution.py:42
  35.9 3.8 %shard_map.60.refs_3_ = bf16[768,1536]{1,0:T(8,128)(2,1)S(1)} custom-call(bf16[256,1536]{1,0:T(8,128)(2,1)S(1)} %pad_maximum_fusion.refs_0_, bf16[256,1536]{1,0:T(8,128)(2,1)S(1)} %collective-permute-done.3.refs_1_, bf16[256,1536]{1,0:T(8,128)(2,1)S(1)} %collective-permute-done.5.refs_2_, bf16[1536,1536]{1,0:T(8,128)(2,1)S(1)} %shard_map.59.refs_3_.refs_2_), custom_call_target="tpu_custom_call" | custom-call | flops 1 | bytes 1 | tf_op jit(solution)/shard_map/pallas_call | solution.py:163
  40.9 3.4 %collective-permute-start.24 = (bf16[128,1536]{1,0:T(8,128)(2,1)S(1)}, bf16[128,1536]{1,0:T(8,128)(2,1)S(1)}, u32[]{:S(2)}, u32[]{:S(2)}) collective-permute-start(bf16[128,1536]{1,0:T(8,128)(2,1)S(1)} %slice.223), channel_id=1, source_target_pairs={{0,96},{1,97},{2,98},{3,99},{4,7},{5,4},{6,5},{7,6},{8,104},{9,105... | collective-permute-start | bytes 1179656 | tf_op jit(solution)/shard_map/ppermute | solution.py:42
  47.7 3.8 %shard_map.65.refs_3_ = bf16[768,1536]{1,0:T(8,128)(2,1)S(1)} custom-call(bf16[256,1536]{1,0:T(8,128)(2,1)S(1)} %pad_maximum_fusion.6.refs_0_, bf16[256,1536]{1,0:T(8,128)(2,1)S(1)} %collective-permute-done.23.refs_1_, bf16[256,1536]{1,0:T(8,128)(2,1)S(1)} %collective-permute-done.25.refs_2_, bf16[1536,1536]{1,0:T(8,128)(2,1)S(1)} %shard_map.62.refs_2_.refs_3_), custom_call_target="tpu_custom_call" | custom-call | flops 1 | bytes 1 | tf_op jit(solution)/shard_map/pallas_call | solution.py:163
  60.7 4.5 %collective-permute-done.9 = bf16[128,1536]{1,0:T(8,128)(2,1)S(1)} collective-permute-done((bf16[128,1536]{1,0:T(8,128)(2,1)S(1)}, bf16[128,1536]{1,0:T(8,128)(2,1)S(1)}, u32[]{:S(2)}, u32[]{:S(2)}) %collective-permute-start.9) | collective-permute-done | bytes 393248 | tf_op jit(solution)/shard_map/ppermute | solution.py:42
  65.8 3.6 %collective-permute-done.29 = bf16[128,1536]{1,0:T(8,128)(2,1)S(1)} collective-permute-done((bf16[128,1536]{1,0:T(8,128)(2,1)S(1)}, bf16[128,1536]{1,0:T(8,128)(2,1)S(1)}, u32[]{:S(2)}, u32[]{:S(2)}) %collective-permute-start.29) | collective-permute-done | bytes 393248 | tf_op jit(solution)/shard_map/ppermute | solution.py:42
  70.0 8.6 %collective-permute-done.10 = bf16[256,1536]{1,0:T(8,128)(2,1)S(1)} collective-permute-done((bf16[256,1536]{1,0:T(8,128)(2,1)S(1)}, bf16[256,1536]{1,0:T(8,128)(2,1)S(1)}, u32[]{:S(2)}, u32[]{:S(2)}) %collective-permute-start.10) | collective-permute-done | bytes 786464 | tf_op jit(solution)/shard_map/ppermute | solution.py:42
  79.0 8.1 %collective-permute-done.30 = bf16[256,1536]{1,0:T(8,128)(2,1)S(1)} collective-permute-done((bf16[256,1536]{1,0:T(8,128)(2,1)S(1)}, bf16[256,1536]{1,0:T(8,128)(2,1)S(1)}, u32[]{:S(2)}, u32[]{:S(2)}) %collective-permute-start.30) | collective-permute-done | bytes 786464 | tf_op jit(solution)/shard_map/ppermute | solution.py:42
  90.2 11.6 %collective-permute-done.12.refs_1_ = bf16[256,1536]{1,0:T(8,128)(2,1)S(1)} collective-permute-done((bf16[256,1536]{1,0:T(8,128)(2,1)S(1)}, bf16[256,1536]{1,0:T(8,128)(2,1)S(1)}, u32[]{:S(2)}, u32[]{:S(2)}) %collective-permute-start.12) | collective-permute-done | bytes 786464 | tf_op jit(solution)/shard_map/ppermute | solution.py:42
  102.1 12.4 %collective-permute-done.14.refs_1_ = bf16[128,1536]{1,0:T(8,128)(2,1)S(1)} collective-permute-done((bf16[128,1536]{1,0:T(8,128)(2,1)S(1)}, bf16[128,1536]{1,0:T(8,128)(2,1)S(1)}, u32[]{:S(2)}, u32[]{:S(2)}) %collective-permute-start.14) | collective-permute-done | bytes 393248 | tf_op jit(solution)/shard_map/ppermute | solution.py:42
  115.5 2.6 %shard_map.67.refs_4_ = bf16[512,1536]{1,0:T(8,128)(2,1)S(1)} custom-call(bf16[256,1536]{1,0:T(8,128)(2,1)S(1)} %multiply_convert_fusion.refs_0_, bf16[256,1536]{1,0:T(8,128)(2,1)S(1)} %collective-permute-done.32.refs_1_, bf16[1536,1536]{1,0:T(8,128)(2,1)S(1)} %shard_map.59.refs_3_.refs_2_), custom_call_target="tpu_custom_call" | custom-call | flops 1 | bytes 1 | tf_op jit(solution)/shard_map/pallas_call | solution.py:163
  120.7 2.8 %shard_map.64 = bf16[1024,1536]{1,0:T(8,128)(2,1)S(1)} custom-call(bf16[256,1536]{1,0:T(8,128)(2,1)S(1)} %collective-permute-done.13.refs_0_, bf16[128,1536]{1,0:T(8,128)(2,1)S(1)} %collective-permute-done.14.refs_1_, bf16[128,1536]{1,0:T(8,128)(2,1)S(1)} %collective-permute-done.15.refs_2_, bf16[1536,1536]{1,0:T(8,128)(2,1)S(1)} %shard_map.62.refs_2_.refs_3_, ...), custom_call_target="tpu_custom_call" | custom-call | flops 1 | bytes 1 | tf_op jit(solution)/shard_map/pallas_call | solution.py:163
  124.1 3.2 %collective-permute-start.18 = (bf16[128,1536]{1,0:T(8,128)(2,1)S(1)}, bf16[128,1536]{1,0:T(8,128)(2,1)S(1)}, u32[]{:S(2)}, u32[]{:S(2)}) collective-permute-start(bf16[128,1536]{1,0:T(8,128)(2,1)S(1)} %get-tuple-element.33), channel_id=1, source_target_pairs={{0,96},{1,97},{2,98},{3,99},{4,7},{5,4},{6,5},{7,6},{8,104},{9,105... | collective-permute-start | bytes 1179656 | tf_op jit(solution)/shard_map/ppermute | solution.py:42
  127.3 2.8 %shard_map.68 = bf16[1024,1536]{1,0:T(8,128)(2,1)S(1)} custom-call(bf16[256,1536]{1,0:T(8,128)(2,1)S(1)} %collective-permute-done.33.refs_0_, bf16[128,1536]{1,0:T(8,128)(2,1)S(1)} %collective-permute-done.34.refs_1_, bf16[128,1536]{1,0:T(8,128)(2,1)S(1)} %collective-permute-done.35.refs_2_, bf16[1536,1536]{1,0:T(8,128)(2,1)S(1)} %shard_map.59.refs_3_.refs_2_, ...), custom_call_target="tpu_custom_call" | custom-call | flops 1 | bytes 1 | tf_op jit(solution)/shard_map/pallas_call | solution.py:163
  130.3 3.2 %collective-permute-start.38 = (bf16[128,1536]{1,0:T(8,128)(2,1)S(1)}, bf16[128,1536]{1,0:T(8,128)(2,1)S(1)}, u32[]{:S(2)}, u32[]{:S(2)}) collective-permute-start(bf16[128,1536]{1,0:T(8,128)(2,1)S(1)} %get-tuple-element.25), channel_id=1, source_target_pairs={{0,96},{1,97},{2,98},{3,99},{4,7},{5,4},{6,5},{7,6},{8,104},{9,105... | collective-permute-start | bytes 1179656 | tf_op jit(solution)/shard_map/ppermute | solution.py:42
  133.9 3.3 %collective-permute-start.19 = (bf16[256,1536]{1,0:T(8,128)(2,1)S(1)}, bf16[256,1536]{1,0:T(8,128)(2,1)S(1)}, u32[]{:S(2)}, u32[]{:S(2)}) collective-permute-start(bf16[256,1536]{1,0:T(8,128)(2,1)S(1)} %pad_maximum_fusion.5), channel_id=1, source_target_pairs={{0,96},{1,97},{2,98},{3,99},{4,7},{5,4},{6,5},{7,6},{8,104},{9,105... | collective-permute-start | bytes 2359304 | tf_op jit(solution)/shard_map/ppermute | solution.py:42
  139.7 3.3 %collective-permute-start.39 = (bf16[256,1536]{1,0:T(8,128)(2,1)S(1)}, bf16[256,1536]{1,0:T(8,128)(2,1)S(1)}, u32[]{:S(2)}, u32[]{:S(2)}) collective-permute-start(bf16[256,1536]{1,0:T(8,128)(2,1)S(1)} %pad_maximum_fusion.10), channel_id=1, source_target_pairs={{0,96},{1,97},{2,98},{3,99},{4,7},{5,4},{6,5},{7,6},{8,104},{9,105... | collective-permute-start | bytes 2359304 | tf_op jit(solution)/shard_map/ppermute | solution.py:42
  143.0 4.7 %collective-permute-done.17 = bf16[256,1536]{1,0:T(8,128)(2,1)S(1)} collective-permute-done((bf16[256,1536]{1,0:T(8,128)(2,1)S(1)}, bf16[256,1536]{1,0:T(8,128)(2,1)S(1)}, u32[]{:S(2)}, u32[]{:S(2)}) %collective-permute-start.17) | collective-permute-done | bytes 786464 | tf_op jit(solution)/shard_map/ppermute | solution.py:42
  151.8 8.5 %collective-permute-done.37 = bf16[256,1536]{1,0:T(8,128)(2,1)S(1)} collective-permute-done((bf16[256,1536]{1,0:T(8,128)(2,1)S(1)}, bf16[256,1536]{1,0:T(8,128)(2,1)S(1)}, u32[]{:S(2)}, u32[]{:S(2)}) %collective-permute-start.37) | collective-permute-done | bytes 786464 | tf_op jit(solution)/shard_map/ppermute | solution.py:42
  164.9 4.8 %collective-permute-done.40 = bf16[64,1536]{1,0:T(8,128)(2,1)S(1)} collective-permute-done((bf16[64,1536]{1,0:T(8,128)(2,1)S(1)}, bf16[64,1536]{1,0:T(8,128)(2,1)S(1)}, u32[]{:S(2)}, u32[]{:S(2)}) %collective-permute-start.40) | collective-permute-done | bytes 196640 | tf_op jit(solution)/shard_map/ppermute | solution.py:42
  (130 shorter events, 45.6 us)
Async XLA Ops:
  1.9 12.4 %collective-permute-start = (bf16[128,1536]{1,0:T(8,128)(2,1)S(1)}, bf16[128,1536]{1,0:T(8,128)(2,1)S(1)}, u32[]{:S(2)}, u32[]{:S(2)}) collective-permute-start(bf16[128,1536]{1,0:T(8,128)(2,1)S(1)} %pad_select_fusion), channel_id=1, source_target_pairs={{0,3},{1,0},{2,1},{3,2},{4,100},{5,101},{6,102},{7,103},{8,11},{9,... | collective-permute-start | bytes 1179656 | tf_op jit(solution)/shard_map/ppermute | solution.py:42
  5.6 12.7 %collective-permute-start.2 = (bf16[128,1536]{1,0:T(8,128)(2,1)S(1)}, bf16[128,1536]{1,0:T(8,128)(2,1)S(1)}, u32[]{:S(2)}, u32[]{:S(2)}) collective-permute-start(bf16[128,1536]{1,0:T(8,128)(2,1)S(1)} %pad_select_fusion), channel_id=1, source_target_pairs={{0,1},{1,2},{2,3},{3,0},{4,36},{5,37},{6,38},{7,39},{8,9},{9,10},{... | collective-permute-start | bytes 1179656 | tf_op jit(solution)/shard_map/ppermute | solution.py:42
  18.4 14.1 %collective-permute-start.5 = (bf16[256,1536]{1,0:T(8,128)(2,1)S(1)}, bf16[256,1536]{1,0:T(8,128)(2,1)S(1)}, u32[]{:S(2)}, u32[]{:S(2)}) collective-permute-start(bf16[256,1536]{1,0:T(8,128)(2,1)S(1)} %pad_maximum_fusion.refs_0_), channel_id=1, source_target_pairs={{0,32},{1,33},{2,34},{3,35},{4,5},{5,6},{6,7},{7,4},{8,40},{9,41},... | collective-permute-start | bytes 2359304 | tf_op jit(solution)/shard_map/ppermute | solution.py:42
  20.3 12.2 %collective-permute-start.3 = (bf16[256,1536]{1,0:T(8,128)(2,1)S(1)}, bf16[256,1536]{1,0:T(8,128)(2,1)S(1)}, u32[]{:S(2)}, u32[]{:S(2)}) collective-permute-start(bf16[256,1536]{1,0:T(8,128)(2,1)S(1)} %pad_maximum_fusion.refs_0_), channel_id=1, source_target_pairs={{0,96},{1,97},{2,98},{3,99},{4,7},{5,4},{6,5},{7,6},{8,104},{9,105... | collective-permute-start | bytes 2359304 | tf_op jit(solution)/shard_map/ppermute | solution.py:42
  22.6 18.2 %collective-permute-start.23 = (bf16[256,1536]{1,0:T(8,128)(2,1)S(1)}, bf16[256,1536]{1,0:T(8,128)(2,1)S(1)}, u32[]{:S(2)}, u32[]{:S(2)}) collective-permute-start(bf16[256,1536]{1,0:T(8,128)(2,1)S(1)} %pad_maximum_fusion.6.refs_0_), channel_id=1, source_target_pairs={{0,96},{1,97},{2,98},{3,99},{4,7},{5,4},{6,5},{7,6},{8,104},{9,105... | collective-permute-start | bytes 2359304 | tf_op jit(solution)/shard_map/ppermute | solution.py:42
  24.6 16.2 %collective-permute-start.25 = (bf16[256,1536]{1,0:T(8,128)(2,1)S(1)}, bf16[256,1536]{1,0:T(8,128)(2,1)S(1)}, u32[]{:S(2)}, u32[]{:S(2)}) collective-permute-start(bf16[256,1536]{1,0:T(8,128)(2,1)S(1)} %pad_maximum_fusion.6.refs_0_), channel_id=1, source_target_pairs={{0,32},{1,33},{2,34},{3,35},{4,5},{5,6},{6,7},{7,4},{8,40},{9,41},... | collective-permute-start | bytes 2359304 | tf_op jit(solution)/shard_map/ppermute | solution.py:42
  32.5 12.6 %collective-permute-start.6 = (bf16[128,1536]{1,0:T(8,128)(2,1)S(1)}, bf16[128,1536]{1,0:T(8,128)(2,1)S(1)}, u32[]{:S(2)}, u32[]{:S(2)}) collective-permute-start(bf16[128,1536]{1,0:T(8,128)(2,1)S(1)} %slice.196), channel_id=1, source_target_pairs={{0,32},{1,33},{2,34},{3,35},{4,5},{5,6},{6,7},{7,4},{8,40},{9,41},... | collective-permute-start | bytes 1179656 | tf_op jit(solution)/shard_map/ppermute | solution.py:42
  32.6 12.5 %collective-permute-start.4 = (bf16[128,1536]{1,0:T(8,128)(2,1)S(1)}, bf16[128,1536]{1,0:T(8,128)(2,1)S(1)}, u32[]{:S(2)}, u32[]{:S(2)}) collective-permute-start(bf16[128,1536]{1,0:T(8,128)(2,1)S(1)} %slice.195), channel_id=1, source_target_pairs={{0,96},{1,97},{2,98},{3,99},{4,7},{5,4},{6,5},{7,6},{8,104},{9,105... | collective-permute-start | bytes 1179656 | tf_op jit(solution)/shard_map/ppermute | solution.py:42
  40.9 10.7 %collective-permute-start.24 = (bf16[128,1536]{1,0:T(8,128)(2,1)S(1)}, bf16[128,1536]{1,0:T(8,128)(2,1)S(1)}, u32[]{:S(2)}, u32[]{:S(2)}) collective-permute-start(bf16[128,1536]{1,0:T(8,128)(2,1)S(1)} %slice.223), channel_id=1, source_target_pairs={{0,96},{1,97},{2,98},{3,99},{4,7},{5,4},{6,5},{7,6},{8,104},{9,105... | collective-permute-start | bytes 1179656 | tf_op jit(solution)/shard_map/ppermute | solution.py:42
  59.1 10.4 %collective-permute-start.29 = (bf16[128,1536]{1,0:T(8,128)(2,1)S(1)}, bf16[128,1536]{1,0:T(8,128)(2,1)S(1)}, u32[]{:S(2)}, u32[]{:S(2)}) collective-permute-start(bf16[128,1536]{1,0:T(8,128)(2,1)S(1)} %get-tuple-element.38), channel_id=1, source_target_pairs={{0,8},{1,9},{2,10},{3,11},{4,28},{5,29},{6,30},{7,31},{8,16},{9,17... | collective-permute-start | bytes 1179656 | tf_op jit(solution)/shard_map/ppermute | solution.py:42
  65.4 13.3 %collective-permute-start.10 = (bf16[256,1536]{1,0:T(8,128)(2,1)S(1)}, bf16[256,1536]{1,0:T(8,128)(2,1)S(1)}, u32[]{:S(2)}, u32[]{:S(2)}) collective-permute-start(bf16[256,1536]{1,0:T(8,128)(2,1)S(1)} %pad_maximum_fusion.1), channel_id=1, source_target_pairs={{0,8},{1,9},{2,10},{3,11},{4,28},{5,29},{6,30},{7,31},{8,16},{9,17... | collective-permute-start | bytes 2359304 | tf_op jit(solution)/shard_map/ppermute | solution.py:42
  69.6 17.5 %collective-permute-start.30 = (bf16[256,1536]{1,0:T(8,128)(2,1)S(1)}, bf16[256,1536]{1,0:T(8,128)(2,1)S(1)}, u32[]{:S(2)}, u32[]{:S(2)}) collective-permute-start(bf16[256,1536]{1,0:T(8,128)(2,1)S(1)} %pad_maximum_fusion.7), channel_id=1, source_target_pairs={{0,8},{1,9},{2,10},{3,11},{4,28},{5,29},{6,30},{7,31},{8,16},{9,17... | collective-permute-start | bytes 2359304 | tf_op jit(solution)/shard_map/ppermute | solution.py:42
  88.6 13.3 %collective-permute-start.12 = (bf16[256,1536]{1,0:T(8,128)(2,1)S(1)}, bf16[256,1536]{1,0:T(8,128)(2,1)S(1)}, u32[]{:S(2)}, u32[]{:S(2)}) collective-permute-start(bf16[256,1536]{1,0:T(8,128)(2,1)S(1)} %get-tuple-element.15.refs_0_), channel_id=1, source_target_pairs={{0,8},{1,9},{2,10},{3,11},{4,28},{5,29},{6,30},{7,31},{8,16},{9,17... | collective-permute-start | bytes 2359304 | tf_op jit(solution)/shard_map/ppermute | solution.py:42
  90.0 24.5 %collective-permute-start.32 = (bf16[256,1536]{1,0:T(8,128)(2,1)S(1)}, bf16[256,1536]{1,0:T(8,128)(2,1)S(1)}, u32[]{:S(2)}, u32[]{:S(2)}) collective-permute-start(bf16[256,1536]{1,0:T(8,128)(2,1)S(1)} %multiply_convert_fusion.refs_0_), channel_id=1, source_target_pairs={{0,8},{1,9},{2,10},{3,11},{4,28},{5,29},{6,30},{7,31},{8,16},{9,17... | collective-permute-start | bytes 2359304 | tf_op jit(solution)/shard_map/ppermute | solution.py:42
  101.9 12.6 %collective-permute-start.14 = (bf16[128,1536]{1,0:T(8,128)(2,1)S(1)}, bf16[128,1536]{1,0:T(8,128)(2,1)S(1)}, u32[]{:S(2)}, u32[]{:S(2)}) collective-permute-start(bf16[128,1536]{1,0:T(8,128)(2,1)S(1)} %slice.262), channel_id=1, source_target_pairs={{0,8},{1,9},{2,10},{3,11},{4,28},{5,29},{6,30},{7,31},{8,16},{9,17... | collective-permute-start | bytes 1179656 | tf_op jit(solution)/shard_map/ppermute | solution.py:42
  102.0 18.7 %collective-permute-start.13 = (bf16[256,1536]{1,0:T(8,128)(2,1)S(1)}, bf16[256,1536]{1,0:T(8,128)(2,1)S(1)}, u32[]{:S(2)}, u32[]{:S(2)}) collective-permute-start(bf16[256,1536]{1,0:T(8,128)(2,1)S(1)} %collective-permute-done.12.refs_1_), channel_id=1, source_target_pairs={{0,4},{1,5},{2,6},{3,7},{4,0},{5,1},{6,2},{7,3},{8,12},{9,13},{10,... | collective-permute-start | bytes 2359304 | tf_op jit(solution)/shard_map/ppermute | solution.py:42
  114.9 12.4 %collective-permute-start.33 = (bf16[256,1536]{1,0:T(8,128)(2,1)S(1)}, bf16[256,1536]{1,0:T(8,128)(2,1)S(1)}, u32[]{:S(2)}, u32[]{:S(2)}) collective-permute-start(bf16[256,1536]{1,0:T(8,128)(2,1)S(1)} %collective-permute-done.32.refs_1_), channel_id=1, source_target_pairs={{0,4},{1,5},{2,6},{3,7},{4,0},{5,1},{6,2},{7,3},{8,12},{9,13},{10,... | collective-permute-start | bytes 2359304 | tf_op jit(solution)/shard_map/ppermute | solution.py:42
  133.8 13.9 %collective-permute-start.17 = (bf16[256,1536]{1,0:T(8,128)(2,1)S(1)}, bf16[256,1536]{1,0:T(8,128)(2,1)S(1)}, u32[]{:S(2)}, u32[]{:S(2)}) collective-permute-start(bf16[256,1536]{1,0:T(8,128)(2,1)S(1)} %pad_maximum_fusion.4), channel_id=1, source_target_pairs={{0,32},{1,33},{2,34},{3,35},{4,5},{5,6},{6,7},{7,4},{8,40},{9,41},... | collective-permute-start | bytes 2359304 | tf_op jit(solution)/shard_map/ppermute | solution.py:42
  133.9 13.8 %collective-permute-start.19 = (bf16[256,1536]{1,0:T(8,128)(2,1)S(1)}, bf16[256,1536]{1,0:T(8,128)(2,1)S(1)}, u32[]{:S(2)}, u32[]{:S(2)}) collective-permute-start(bf16[256,1536]{1,0:T(8,128)(2,1)S(1)} %pad_maximum_fusion.5), channel_id=1, source_target_pairs={{0,96},{1,97},{2,98},{3,99},{4,7},{5,4},{6,5},{7,6},{8,104},{9,105... | collective-permute-start | bytes 2359304 | tf_op jit(solution)/shard_map/ppermute | solution.py:42
  139.5 20.8 %collective-permute-start.37 = (bf16[256,1536]{1,0:T(8,128)(2,1)S(1)}, bf16[256,1536]{1,0:T(8,128)(2,1)S(1)}, u32[]{:S(2)}, u32[]{:S(2)}) collective-permute-start(bf16[256,1536]{1,0:T(8,128)(2,1)S(1)} %pad_maximum_fusion.9), channel_id=1, source_target_pairs={{0,32},{1,33},{2,34},{3,35},{4,5},{5,6},{6,7},{7,4},{8,40},{9,41},... | collective-permute-start | bytes 2359304 | tf_op jit(solution)/shard_map/ppermute | solution.py:42
  139.7 20.7 %collective-permute-start.39 = (bf16[256,1536]{1,0:T(8,128)(2,1)S(1)}, bf16[256,1536]{1,0:T(8,128)(2,1)S(1)}, u32[]{:S(2)}, u32[]{:S(2)}) collective-permute-start(bf16[256,1536]{1,0:T(8,128)(2,1)S(1)} %pad_maximum_fusion.10), channel_id=1, source_target_pairs={{0,96},{1,97},{2,98},{3,99},{4,7},{5,4},{6,5},{7,6},{8,104},{9,105... | collective-permute-start | bytes 2359304 | tf_op jit(solution)/shard_map/ppermute | solution.py:42
  148.0 14.3 %collective-permute-start.20 = (bf16[64,1536]{1,0:T(8,128)(2,1)S(1)}, bf16[64,1536]{1,0:T(8,128)(2,1)S(1)}, u32[]{:S(2)}, u32[]{:S(2)}) collective-permute-start(bf16[64,1536]{1,0:T(8,128)(2,1)S(1)} %get-tuple-element.49), channel_id=1, source_target_pairs={{0,1},{1,2},{2,3},{3,0},{4,36},{5,37},{6,38},{7,39},{8,9},{9,10},{... | collective-permute-start | bytes 589832 | tf_op jit(solution)/shard_map/ppermute | solution.py:42
  148.4 15.8 %collective-permute-start.21 = (bf16[64,1536]{1,0:T(8,128)(2,1)S(1)}, bf16[64,1536]{1,0:T(8,128)(2,1)S(1)}, u32[]{:S(2)}, u32[]{:S(2)}) collective-permute-start(bf16[64,1536]{1,0:T(8,128)(2,1)S(1)} %get-tuple-element.51), channel_id=1, source_target_pairs={{0,2},{1,3},{2,0},{3,1},{4,68},{5,69},{6,70},{7,71},{8,10},{9,11},... | collective-permute-start | bytes 589832 | tf_op jit(solution)/shard_map/ppermute | solution.py:42
  150.4 13.8 %collective-permute-start.22 = (bf16[64,1536]{1,0:T(8,128)(2,1)S(1)}, bf16[64,1536]{1,0:T(8,128)(2,1)S(1)}, u32[]{:S(2)}, u32[]{:S(2)}) collective-permute-start(bf16[64,1536]{1,0:T(8,128)(2,1)S(1)} %get-tuple-element.50), channel_id=1, source_target_pairs={{0,3},{1,0},{2,1},{3,2},{4,100},{5,101},{6,102},{7,103},{8,11},{9,... | collective-permute-start | bytes 589832 | tf_op jit(solution)/shard_map/ppermute | solution.py:42
  (24 other events, 187.1 us)
